TPU v7x, 128 devices: a whole 4x4x4 slice. The times are simulated.
128 devices in a mesh: section: 4 (over y), seq: 32 (over z, x, core).
Axes of the slice: x: 4, y: 4, z: 4, core: 2. Of those that a mesh axis runs over, the one named last changes fastest.
Arguments:
- patch_in: bfloat16 [4, 2, 2048, 2432], P('section', None, 'seq'), may hold values from -6 to 6
- modulation: float32 [4, 3, 2432], P('section'), may hold values from -3 to 3
- qkv_weight: bfloat16 [4, 2432, 6144], P('section', None, 'seq'), may hold values from -0.125 to 0.125
- qk_gain: float32 [4, 2, 64], P('section'), may hold values from 0.1 to 1.9
- out_weight: bfloat16 [4, 2048, 2432], P('section'), may hold values from -0.125 to 0.125
- kv_cache: bfloat16 [4, 2, 8192, 4096], P('section', None, None, 'seq'), may hold values from -190 to 190
- text_kv: bfloat16 [4, 2, 256, 4096], P('section', None, None, 'seq'), may hold values from -6 to 6
- patch_offsets: int32 [4], replicated, may hold values from 0 to 6144, as said below
- step_index: int32 [1], replicated, may hold values from 0 to 3
- text_count: int32 [2], replicated, may hold values from 64 to 256, as said below
Outputs:
- patch_out: bfloat16 [4, 2, 2048, 2432], P('section', None, 'seq')
- fresh_kv: bfloat16 [4, 2, 2048, 4096], P('section', None, None, 'seq')
Inputs may be any that keep to these rules, and one draw needn't show every extreme that they name: `patch_offsets`: a permutation of the multiples of 2048 below 8192. `text_count`: in every draw one of the two branches uses all 256 text slots.
All inputs are finite; a program needn't handle non-finite values.
Results may differ from a plain program's by a relative error of at most 0.0017.
The roundings to bfloat16 on the way count: a program that leaves them out, or rounds other values in their place, can miss the bound.
Values may be sent and summed in bfloat16 or wider, within the bound.
No kernel may reach another device: no remote copies, remote signals or barrier semaphores. Data moves between devices by JAX's collectives and lax.ppermute only.
A program may use at most 128 MiB of HBM per device.

v0:
```python
import math

import jax
import jax.numpy as jnp
from jax import lax
from jax.sharding import PartitionSpec as P

HD = 64


def passed_along(value, axis, steps):
    count = lax.axis_size(axis)
    pairs = [(source, (source + steps) % count) for source in range(count)]
    return lax.ppermute(value, axis, pairs)


def modulated(entering, mod_rows):
    values = entering.astype(jnp.float32)
    center = jnp.mean(values, axis=-1, keepdims=True)
    spread = jnp.mean((values - center) ** 2, axis=-1, keepdims=True)
    normal_rows = (values - center) * lax.rsqrt(spread + 1e-06)
    return (normal_rows * (1.0 + mod_rows[1]) + mod_rows[0]).astype(jnp.bfloat16)


def normalize_heads(projected, gains):
    head_size = gains.shape[-1]
    shaped = projected.reshape(projected.shape[0], projected.shape[1], -1, 3, head_size)
    queries = shaped[:, :, :, 0, :]
    keys_new = shaped[:, :, :, 1, :]
    values_new = shaped[:, :, :, 2, :]
    queries = (
        queries * lax.rsqrt(jnp.mean(queries * queries, axis=-1, keepdims=True) + 1e-06) * gains[0]
    )
    keys_new = (
        keys_new
        * lax.rsqrt(jnp.mean(keys_new * keys_new, axis=-1, keepdims=True) + 1e-06)
        * gains[1]
    )
    joined = jnp.stack([queries, keys_new, values_new], axis=3).astype(jnp.bfloat16)
    return joined.reshape(projected.shape)


def attend(mixed, cache, text_part, offset, counts):
    batch, rows_all, packed = mixed.shape
    heads_here = packed // (3 * HD)
    shaped = mixed.reshape(batch, rows_all, heads_here, 3, HD)
    fresh = shaped[:, :, :, 1:, :].reshape(batch, rows_all, heads_here * 2 * HD)
    zero_index = jnp.zeros((), jnp.int32)
    keys_image = lax.dynamic_update_slice(cache, fresh, (zero_index, offset, zero_index))
    every_key = jnp.concatenate([keys_image, text_part], axis=1)
    key_count = every_key.shape[1]
    image_rows = cache.shape[1]
    every_key = every_key.reshape(batch, key_count, heads_here, 2, HD)
    key_vecs = every_key[:, :, :, 0, :]
    value_vecs = every_key[:, :, :, 1, :]
    positions = jnp.arange(key_count, dtype=jnp.int32)
    usable = (positions[None, :] < image_rows) | (positions[None, :] - image_rows < counts[:, None])
    block_rows = math.gcd(rows_all, 512)
    blocks = rows_all // block_rows
    queries = (
        shaped[:, :, :, 0, :]
        .reshape(batch, blocks, block_rows, heads_here, HD)
        .transpose(1, 0, 2, 3, 4)
    )

    def block_attend(query_block):
        scores = jnp.einsum(
            "bqhd,bkhd->bhqk", query_block, key_vecs, preferred_element_type=jnp.float32
        ) * HD ** (-0.5)
        scores = jnp.where(usable[:, None, None, :], scores, -1e30)
        highest = jnp.max(scores, axis=-1, keepdims=True)
        raised = jnp.exp(scores - highest)
        totals = jnp.sum(raised, axis=-1, keepdims=True)
        probs = (raised / totals).astype(jnp.bfloat16)
        result = jnp.einsum(
            "bhqk,bkhd->bqhd", probs, value_vecs, preferred_element_type=jnp.float32
        )
        return result.astype(jnp.bfloat16)

    attended = lax.map(block_attend, queries)
    attended = attended.transpose(1, 0, 2, 3, 4).reshape(batch, rows_all, heads_here * HD)
    return (attended, fresh)


def local(
    patch_in,
    modulation,
    qkv_weight,
    qk_gain,
    out_weight,
    kv_cache,
    text_kv,
    patch_offsets,
    step_index,
    text_count,
):
    section_index = lax.axis_index("section")
    patch_total = patch_offsets.shape[0]
    patch_number = (step_index[0] - section_index) % patch_total
    offset = jnp.sum(
        jnp.where(jnp.arange(patch_total, dtype=jnp.int32) == patch_number, patch_offsets, 0)
    )
    entering = patch_in[0]
    rows_here = entering.shape[1]
    model_width = entering.shape[2]
    normed = modulated(entering, modulation[0])
    flat_rows = normed.reshape(2 * rows_here, model_width)
    projected = jnp.dot(
        flat_rows,
        lax.all_gather(qkv_weight[0], "seq", axis=1, tiled=True),
        preferred_element_type=jnp.float32,
    )
    packed_local = normalize_heads(projected.reshape(2, rows_here, -1), qk_gain[0])
    mixed = lax.all_to_all(packed_local, "seq", split_axis=2, concat_axis=1, tiled=True)
    attended, fresh = attend(mixed, kv_cache[0], text_kv[0], offset, text_count)
    joined = lax.all_to_all(attended, "seq", split_axis=1, concat_axis=2, tiled=True)
    projected_out = jnp.dot(
        joined.reshape(2 * rows_here, -1), out_weight[0], preferred_element_type=jnp.float32
    )
    block_out = entering.astype(jnp.float32) + modulation[0, 2] * projected_out.reshape(
        2, rows_here, model_width
    )
    moved = passed_along(block_out.astype(jnp.bfloat16), "section", 1)
    return (moved[None], fresh[None])


def solution(mesh):
    in_specs = (
        P("section", None, "seq", None),
        P("section", None, None),
        P("section", None, "seq"),
        P("section", None, None),
        P("section", None, None),
        P("section", None, None, "seq"),
        P("section", None, None, "seq"),
        P(),
        P(),
        P(),
    )
    out_specs = (P("section", None, "seq", None), P("section", None, None, "seq"))
    return jax.shard_map(local, mesh=mesh, in_specs=in_specs, out_specs=out_specs, check_vma=False)
```

profile of v0, /device:TPU:1, one launch (start us, length us, event | category | flops | bytes accessed | tf_op | source)
XLA Modules:
  0.0 456.1 jit_solution(10169525363772976198)
XLA Ops:
  12.7 105.6 %all-gather.3.cloned.1.call-done = bf16[1,2432,6144]{1,2,0:T(8,128)(2,1)} async-done(((bf16[1,2432,192]{1,2,0:T(8,128)(2,1)}), bf16[1,2432,6144]{1,2,0:T(8,128)(2,1)}) %all-gather.3.cloned.1.call-update) | async-done | bytes 29884432 | tf_op jit(solution)/shard_map/all_gather | solution.py:110
  118.3 16.0 %fusion.44 = f32[2,64,32,3,64]{1,4,3,2,0:T(8,128)S(1)} fusion(bf16[32,3,64,2432,1]{3,2,1,0,4:T(8,128)(2,1)} %bitcast.134, bf16[1,2,64,2432]{3,2,1,0:T(8,128)(2,1)} %param.12, f32[2432]{0:T(1024)S(1)} %get-tuple-element.89, f32[2432]{0:T(1024)S(1)} %get-tuple-element.90, f32[2,64]{1,0:T(2,128)S(1)} %add_rsqrt_fusion.2, f32[2,64]{1,0:T(2,128)S(1)} %broadcast_multiply_fusion), kind=kOutput, calls=%fused_computation.49 | convolution fusion | flops 3827073024 | bytes 33673216 | tf_op jit(solution)/shard_map/dot_general | solution.py:108
  136.9 26.7 %copy.50 = bf16[2,64,6144]{1,0,2:T(2,128)(2,1)S(1)} copy(bf16[2,64,6144]{1,2,0:T(8,128)(2,1)S(1)} %bitcast.121) | data formatting | bytes 3145728 | tf_op jit(solution)/shard_map/convert_element_type | solution.py:39
  166.8 5.3 %all-to-all-start = ((bf16[32,2,12288]{2,1,0:T(2,128)(2,1)}), bf16[32,2,12288]{2,1,0:T(2,128)(2,1)}, u32[]{:S(2)}, u32[]{:S(2)}) async-start(bf16[32,2,12288]{2,1,0:T(2,128)(2,1)} %reshape.166), calls=%async_computation | async-start | bytes 3145728 | tf_op jit(solution)/shard_map/all_to_all | solution.py:114
  174.7 6.4 %copy.30 = bf16[1,2,8192,128]{2,3,1,0:T(8,128)(2,1)} copy(bf16[1,2,8192,128]{3,2,1,0:T(8,128)(2,1)} %param.17) | data formatting | bytes 8388608 | tf_op args[5]
  181.9 12.3 %all-to-all-done = bf16[32,2,12288]{2,1,0:T(2,128)(2,1)} async-done(((bf16[32,2,12288]{2,1,0:T(2,128)(2,1)}), bf16[32,2,12288]{2,1,0:T(2,128)(2,1)}, u32[]{:S(2)}, u32[]{:S(2)}) %all-to-all-start) | async-done | bytes 1572896 | tf_op jit(solution)/shard_map/all_to_all | solution.py:114
  194.2 7.0 %reshape.167 = bf16[6144,2,64]{2,1,0:T(2,128)(2,1)S(1)} reshape(bf16[32,2,12288]{2,1,0:T(2,128)(2,1)} %all-to-all-done) | data formatting | bytes 3145728
  210.2 10.0 %dynamic_update_slice.7 = bf16[2,8192,128]{1,2,0:T(8,128)(2,1)} dynamic-update-slice(bf16[2,8192,128]{1,2,0:T(8,128)(2,1)} %bitcast.119, bf16[2,2048,128]{1,2,0:T(8,128)(2,1)S(1)} %bitcast.125, s32[]{:T(128)} %copy.62, s32[]{:T(128)S(6)} %select_n.21, s32[]{:T(128)} %copy.62) | dynamic-update-slice | bytes 2097156 | tf_op jit(solution)/shard_map/dynamic_update_slice | solution.py:49
  223.6 181.1 %while.11 = (s32[]{:T(128)}, bf16[4,2,512,1,64]{2,4,1,3,0:T(8,128)(2,1)}, bf16[4,2,512,1,64]{2,4,1,3,0:T(8,128)(2,1)S(1)}, bf16[2,8448,1,64]{1,3,0,2:T(8,128)(2,...) while((s32[]{:T(128)}, ...), condition=%wide.region_8.9_spmd.clone, body=%wide.region_5.8_spmd.clone.sunk | while | flops 2318498816 | bytes 108544360 | solution.py:80
  223.7 13.6 %fusion.58 = (f32[2,512]{1,0:T(2,128)S(1)}, f32[2,512,8448]{2,1,0:T(8,128)}) fusion(pred[2,8448]{1,0:T(4,128)(4,1)S(1)} %compare_or_fusion.2, bf16[2,8448,1,64]{1,3,0,2:T(8,128)(2,1)S(1)} %get-tuple-element.191, bf16[4,2,512,1,64]{2,4,1,3,0:T(8,128)(2,1)S(1)} %get-tuple-element.190, s32[]{:T(128)} %get-tuple-element.179), kind=kOutput, calls=%fused_computation.4.clone.1 | convolution fusion | flops 1133247488 | bytes 36934660 | tf_op jit(solution)/shard_map/while/body/eval_jaxpr/bqhd,bkhd->bhqk/dot_general | solution.py:67
  237.3 15.3 %fusion.59 = f32[2,512]{1,0:T(2,128)S(1)} fusion(f32[2,512,8448]{2,1,0:T(8,128)} %get-tuple-element.168, f32[2,512]{1,0:T(2,128)S(1)} %get-tuple-element.169, pred[2,8448]{1,0:T(4,128)(4,1)S(1)} %compare_or_fusion.2), kind=kLoop, calls=%fused_computation.5.clone.1 | loop fusion | flops 34601984 | bytes 34628096 | tf_op jit(solution)/shard_map/while/body/eval_jaxpr/reduce_sum | solution.py:73
  252.6 16.2 %fusion.60 = bf16[4,2,512,1,64]{2,4,1,3,0:T(8,128)(2,1)} fusion(bf16[4,2,512,1,64]{2,4,1,3,0:T(8,128)(2,1)} %get-tuple-element.180, s32[]{:T(128)} %get-tuple-element.179, bf16[2,8448,1,64]{1,3,0,2:T(8,128)(2,1)} %get-tuple-element.192, f32[2,512,8448]{2,1,0:T(8,128)} %get-tuple-element.168, f32[2,512]{1,0:T(2,128)S(1)} %fusion.59, ...), kind=kOutput, calls=%fused_computation.12.clone.1 | convolution fusion | flops 1150615552 | bytes 36922368 | tf_op jit(solution)/shard_map/while/body/eval_jaxpr/bhqk,bkhd->bqhd/dot_general | solution.py:75
  269.0 13.6 %fusion.58 = (f32[2,512]{1,0:T(2,128)S(1)}, f32[2,512,8448]{2,1,0:T(8,128)}) fusion(pred[2,8448]{1,0:T(4,128)(4,1)S(1)} %compare_or_fusion.2, bf16[2,8448,1,64]{1,3,0,2:T(8,128)(2,1)S(1)} %get-tuple-element.191, bf16[4,2,512,1,64]{2,4,1,3,0:T(8,128)(2,1)S(1)} %get-tuple-element.190, s32[]{:T(128)} %get-tuple-element.179), kind=kOutput, calls=%fused_computation.4.clone.1 | convolution fusion | flops 1133247488 | bytes 36934660 | tf_op jit(solution)/shard_map/while/body/eval_jaxpr/bqhd,bkhd->bhqk/dot_general | solution.py:67
  282.6 15.3 %fusion.59 = f32[2,512]{1,0:T(2,128)S(1)} fusion(f32[2,512,8448]{2,1,0:T(8,128)} %get-tuple-element.168, f32[2,512]{1,0:T(2,128)S(1)} %get-tuple-element.169, pred[2,8448]{1,0:T(4,128)(4,1)S(1)} %compare_or_fusion.2), kind=kLoop, calls=%fused_computation.5.clone.1 | loop fusion | flops 34601984 | bytes 34628096 | tf_op jit(solution)/shard_map/while/body/eval_jaxpr/reduce_sum | solution.py:73
  297.9 16.2 %fusion.60 = bf16[4,2,512,1,64]{2,4,1,3,0:T(8,128)(2,1)} fusion(bf16[4,2,512,1,64]{2,4,1,3,0:T(8,128)(2,1)} %get-tuple-element.180, s32[]{:T(128)} %get-tuple-element.179, bf16[2,8448,1,64]{1,3,0,2:T(8,128)(2,1)} %get-tuple-element.192, f32[2,512,8448]{2,1,0:T(8,128)} %get-tuple-element.168, f32[2,512]{1,0:T(2,128)S(1)} %fusion.59, ...), kind=kOutput, calls=%fused_computation.12.clone.1 | convolution fusion | flops 1150615552 | bytes 36922368 | tf_op jit(solution)/shard_map/while/body/eval_jaxpr/bhqk,bkhd->bqhd/dot_general | solution.py:75
  314.2 13.6 %fusion.58 = (f32[2,512]{1,0:T(2,128)S(1)}, f32[2,512,8448]{2,1,0:T(8,128)}) fusion(pred[2,8448]{1,0:T(4,128)(4,1)S(1)} %compare_or_fusion.2, bf16[2,8448,1,64]{1,3,0,2:T(8,128)(2,1)S(1)} %get-tuple-element.191, bf16[4,2,512,1,64]{2,4,1,3,0:T(8,128)(2,1)S(1)} %get-tuple-element.190, s32[]{:T(128)} %get-tuple-element.179), kind=kOutput, calls=%fused_computation.4.clone.1 | convolution fusion | flops 1133247488 | bytes 36934660 | tf_op jit(solution)/shard_map/while/body/eval_jaxpr/bqhd,bkhd->bhqk/dot_general | solution.py:67
  327.8 15.3 %fusion.59 = f32[2,512]{1,0:T(2,128)S(1)} fusion(f32[2,512,8448]{2,1,0:T(8,128)} %get-tuple-element.168, f32[2,512]{1,0:T(2,128)S(1)} %get-tuple-element.169, pred[2,8448]{1,0:T(4,128)(4,1)S(1)} %compare_or_fusion.2), kind=kLoop, calls=%fused_computation.5.clone.1 | loop fusion | flops 34601984 | bytes 34628096 | tf_op jit(solution)/shard_map/while/body/eval_jaxpr/reduce_sum | solution.py:73
  343.2 16.2 %fusion.60 = bf16[4,2,512,1,64]{2,4,1,3,0:T(8,128)(2,1)} fusion(bf16[4,2,512,1,64]{2,4,1,3,0:T(8,128)(2,1)} %get-tuple-element.180, s32[]{:T(128)} %get-tuple-element.179, bf16[2,8448,1,64]{1,3,0,2:T(8,128)(2,1)} %get-tuple-element.192, f32[2,512,8448]{2,1,0:T(8,128)} %get-tuple-element.168, f32[2,512]{1,0:T(2,128)S(1)} %fusion.59, ...), kind=kOutput, calls=%fused_computation.12.clone.1 | convolution fusion | flops 1150615552 | bytes 36922368 | tf_op jit(solution)/shard_map/while/body/eval_jaxpr/bhqk,bkhd->bqhd/dot_general | solution.py:75
  359.5 13.6 %fusion.58 = (f32[2,512]{1,0:T(2,128)S(1)}, f32[2,512,8448]{2,1,0:T(8,128)}) fusion(pred[2,8448]{1,0:T(4,128)(4,1)S(1)} %compare_or_fusion.2, bf16[2,8448,1,64]{1,3,0,2:T(8,128)(2,1)S(1)} %get-tuple-element.191, bf16[4,2,512,1,64]{2,4,1,3,0:T(8,128)(2,1)S(1)} %get-tuple-element.190, s32[]{:T(128)} %get-tuple-element.179), kind=kOutput, calls=%fused_computation.4.clone.1 | convolution fusion | flops 1133247488 | bytes 36934660 | tf_op jit(solution)/shard_map/while/body/eval_jaxpr/bqhd,bkhd->bhqk/dot_general | solution.py:67
  373.1 15.3 %fusion.59 = f32[2,512]{1,0:T(2,128)S(1)} fusion(f32[2,512,8448]{2,1,0:T(8,128)} %get-tuple-element.168, f32[2,512]{1,0:T(2,128)S(1)} %get-tuple-element.169, pred[2,8448]{1,0:T(4,128)(4,1)S(1)} %compare_or_fusion.2), kind=kLoop, calls=%fused_computation.5.clone.1 | loop fusion | flops 34601984 | bytes 34628096 | tf_op jit(solution)/shard_map/while/body/eval_jaxpr/reduce_sum | solution.py:73
  388.4 16.2 %fusion.60 = bf16[4,2,512,1,64]{2,4,1,3,0:T(8,128)(2,1)} fusion(bf16[4,2,512,1,64]{2,4,1,3,0:T(8,128)(2,1)} %get-tuple-element.180, s32[]{:T(128)} %get-tuple-element.179, bf16[2,8448,1,64]{1,3,0,2:T(8,128)(2,1)} %get-tuple-element.192, f32[2,512,8448]{2,1,0:T(8,128)} %get-tuple-element.168, f32[2,512]{1,0:T(2,128)S(1)} %fusion.59, ...), kind=kOutput, calls=%fused_computation.12.clone.1 | convolution fusion | flops 1150615552 | bytes 36922368 | tf_op jit(solution)/shard_map/while/body/eval_jaxpr/bhqk,bkhd->bqhd/dot_general | solution.py:75
  407.8 16.5 %all_to_all.30 = bf16[32,2,4096]{2,1,0:T(2,128)(2,1)S(1)} all-to-all(bf16[32,2,4096]{2,1,0:T(2,128)(2,1)S(1)} %reshape.168), channel_id=1, replica_groups=mesh['section'=4,'seq'=32] {'seq'}, dimensions={0} | all-to-all | bytes 1048576 | tf_op jit(solution)/shard_map/all_to_all | solution.py:116
  426.5 5.5 %fusion.30 = bf16[2,64,2432]{2,1,0:T(8,128)(2,1)S(1)} fusion(bf16[2,64,2048]{2,1,0:T(8,128)(2,1)S(1)} %dot_general.21, bf16[1,2048,2432]{2,1,0:T(8,128)(2,1)} %param.16, bf16[1,2,64,2432]{3,2,1,0:T(8,128)(2,1)S(1)} %copy-done.2, f32[2432]{0:T(1024)S(1)} %copy-done.4), kind=kOutput, calls=%fused_computation.25 | convolution fusion | flops 1276313600 | bytes 11740672 | tf_op jit(solution)/shard_map/dot_general | solution.py:117
  434.5 13.9 %collective-permute-done = bf16[2,64,2432]{2,1,0:T(8,128)(2,1)S(1)} collective-permute-done((bf16[2,64,2432]{2,1,0:T(8,128)(2,1)S(1)}, bf16[2,64,2432]{2,1,0:T(8,128)(2,1)S(1)}, u32[]{:S(2)}, u32[]{:S(2)}) %collective-permute-start) | collective-permute-done | bytes 622624 | tf_op jit(solution)/shard_map/ppermute | solution.py:14
  (52 shorter events, 33.4 us)
Async XLA Ops:
  7.2 111.2 %all-gather.3.cloned.1.call-start = ((), (), s32[]{:S(2)}) async-start(), calls=%async_computation.2 | async-start | bytes 30818304 | tf_op jit(solution)/shard_map/all_gather | solution.py:110
  163.6 9.2 %copy-start.6 = (s32[4]{0:T(128)S(1)}, s32[4]{0:T(128)}, u32[]{:S(2)}) copy-start(s32[4]{0:T(128)} %param.19) | copy-start | bytes 52
  166.8 27.4 %all-to-all-start = ((bf16[32,2,12288]{2,1,0:T(2,128)(2,1)}), bf16[32,2,12288]{2,1,0:T(2,128)(2,1)}, u32[]{:S(2)}, u32[]{:S(2)}) async-start(bf16[32,2,12288]{2,1,0:T(2,128)(2,1)} %reshape.166), calls=%async_computation | async-start | bytes 3145728 | tf_op jit(solution)/shard_map/all_to_all | solution.py:114
  174.7 6.4 %copy-start.3 = (bf16[1,2,256,128]{3,2,1,0:T(8,128)(2,1)S(1)}, bf16[1,2,256,128]{3,2,1,0:T(8,128)(2,1)}, u32[]{:S(2)}) copy-start(bf16[1,2,256,128]{3,2,1,0:T(8,128)(2,1)} %param.18) | copy-start | bytes 393220
  209.7 10.5 %copy-start = (bf16[2,2048,1,2,64]{1,4,3,0,2:T(8,128)(2,1)}, bf16[2,2048,1,2,64]{1,4,3,0,2:T(8,128)(2,1)S(1)}, u32[]{:S(2)}) copy-start(bf16[2,2048,1,2,64]{1,4,3,0,2:T(8,128)(2,1)S(1)} %slice.57) | copy-start | bytes 3145732
  220.2 3.3 copy-start.5
  407.7 18.7 %copy-start.2 = (bf16[1,2,64,2432]{3,2,1,0:T(8,128)(2,1)S(1)}, bf16[1,2,64,2432]{3,2,1,0:T(8,128)(2,1)}, u32[]{:S(2)}) copy-start(bf16[1,2,64,2432]{3,2,1,0:T(8,128)(2,1)} %param.12) | copy-start | bytes 1867780
  407.8 18.7 %copy-start.4 = (f32[2432]{0:T(1024)S(1)}, f32[2432]{0:T(1024)}, u32[]{:S(2)}) copy-start(f32[2432]{0:T(1024)} %get-tuple-element.88) | copy-start | bytes 29188
  426.5 6.8 %copy-start.1 = (bf16[2,2048,1,2,64]{1,4,3,0,2:T(8,128)(2,1)S(1)}, bf16[2,2048,1,2,64]{1,4,3,0,2:T(8,128)(2,1)}, u32[]{:S(2)}) copy-start(bf16[2,2048,1,2,64]{1,4,3,0,2:T(8,128)(2,1)} %copy-done) | copy-start | bytes 3145732
  432.0 16.4 %collective-permute-start = (bf16[2,64,2432]{2,1,0:T(8,128)(2,1)S(1)}, bf16[2,64,2432]{2,1,0:T(8,128)(2,1)S(1)}, u32[]{:S(2)}, u32[]{:S(2)}) collective-permute-start(bf16[2,64,2432]{2,1,0:T(8,128)(2,1)S(1)} %fusion.30), channel_id=1, source_target_pairs={{0,32},{32,64},{64,96},{96,0},{1,33},{33,65},{65,97},{97,1},{2,34}... | collective-permute-start | bytes 1867784 | tf_op jit(solution)/shard_map/ppermute | solution.py:14
Sparse Core Ops, SparseCore 0:
  10.3 108.0 all-gather.2
where the time goes:
time: 458 us; the launch traced here: 456 us
  matrix products  141 us (31%)
  waiting for transfers between devices  132 us (29%)
  other arithmetic  72.1 us (16%)
  local copies, waits for them, and re-layouts  70.7 us (15%)
  between operations  16.9 us (4%)
  blocking collectives  16.5 us (4%)
  starting transfers between devices  6.6 us (1%)
    all_gather x1, waiting for transfers between devices, local(): lax.all_gather(qkv_weight[0], 'seq', axis=1, tiled=True)  106 us
    dot_general x4, matrix products, block_attend(): jnp.einsum('bhqk,bkhd->bqhd', probs, value_vecs, preferred_element_type=j...  64.8 us
    reduce_sum x4, other arithmetic, block_attend(): totals = jnp.sum(raised, axis=-1, keepdims=True)  61.3 us
    dot_general x4, matrix products, block_attend(): jnp.einsum('bqhd,bkhd->bhqk', query_block, key_vecs, preferred_element_ty...  54.5 us
    convert_element_type x1, local copies, waits for them, and re-layouts, normalize_heads(): jnp.stack([queries, keys_new, values_new], axis=3).astype(jnp.bfloat16)  26.7 us
    unnamed x23, local copies, waits for them, and re-layouts  20.4 us
    all_to_all x1, blocking collectives, local(): lax.all_to_all(attended, 'seq', split_axis=1, concat_axis=2, tiled=True)  16.5 us
    dot_general x1, matrix products, local(): jnp.dot(flat_rows, lax.all_gather(qkv_weight[0], 'seq', axis=1, tiled=Tru...  16 us
  transfers between devices with their start and end apart: 3, of which 3 were waited for; matrix products, arithmetic and copies ran while one was open for 3% of the time, Pallas kernels for 0%

commit v1 on v0

v1 whole, which is shorter than its diff:
```python
import functools
import math

import jax
import jax.numpy as jnp
from jax import lax
from jax.experimental import pallas as pl
from jax.experimental.pallas import tpu as pltpu
from jax.sharding import PartitionSpec as P

HD = 64
SIDE = 4
CHIPS = SIDE * SIDE
STEPS = (0, 1, -1, 2)
MIB = 2**20


def pairs_of(phase, step):
    pairs = []
    for z in range(SIDE):
        for x in range(SIDE):
            for core in range(2):
                if (phase + core) % 2 == 0:
                    to = (z * SIDE + (x + step) % SIDE) * 2 + core
                else:
                    to = (((z + step) % SIDE) * SIDE + x) * 2 + core
                pairs.append(((z * SIDE + x) * 2 + core, to))
    return pairs


def along(value, phase, step):
    return lax.ppermute(value, "seq", pairs_of(phase, step))


def swapped(value):
    return lax.ppermute(value, "seq", [(i, i ^ 1) for i in range(2 * CHIPS)])


def after(value, *others):
    return lax.optimization_barrier((value, *others))[0]


def norm_kernel(x_ref, mod_ref, out_ref):
    shift = mod_ref[0:1, :]
    scale = 1.0 + mod_ref[1:2, :]
    rows = x_ref.shape[1]
    for branch in range(2):
        values = x_ref[branch].astype(jnp.float32)
        center = jnp.mean(values, axis=-1, keepdims=True)
        moved = values - center
        spread = jnp.mean(moved * moved, axis=-1, keepdims=True)
        out_ref[branch * rows : (branch + 1) * rows, :] = (
            moved * lax.rsqrt(spread + 1e-06) * scale + shift
        ).astype(jnp.bfloat16)


def normed_rows(entering, mod_rows):
    rows, width = entering.shape[1:]
    return pl.pallas_call(
        norm_kernel,
        out_shape=jax.ShapeDtypeStruct((2 * rows, width), jnp.bfloat16),
        compiler_params=pltpu.CompilerParams(vmem_limit_bytes=16 * MIB),
    )(entering, mod_rows)


def pack_kernel(own, other, out_ref):
    for at, weight in ((0, own), (4 * HD, other)):
        out_ref[at : at + 2 * HD, :] = weight[HD:, :]
        out_ref[at + 2 * HD : at + 3 * HD, :] = weight[:HD, :]
        out_ref[at + 3 * HD : at + 4 * HD, :] = jnp.zeros((HD, out_ref.shape[1]), out_ref.dtype)


def packed_rows(own, other):
    return pl.pallas_call(
        pack_kernel,
        out_shape=jax.ShapeDtypeStruct((8 * HD, own.shape[1]), own.dtype),
        compiler_params=pltpu.CompilerParams(vmem_limit_bytes=16 * MIB),
    )(own, other)


def split_kernel(*refs):
    parts, outs = refs[:-2], refs[-2:]
    rows = parts[0].shape[0] // 2
    for branch, out_ref in enumerate(outs):
        for i, part in enumerate(parts):
            out_ref[i * rows : (i + 1) * rows, :] = part[branch * rows : (branch + 1) * rows, :]


def split_rows(parts):
    rows, width = parts[0].shape
    out = jax.ShapeDtypeStruct((rows // 2 * len(parts), width), parts[0].dtype)
    return pl.pallas_call(
        split_kernel,
        out_shape=(out, out),
        compiler_params=pltpu.CompilerParams(vmem_limit_bytes=24 * MIB),
    )(*parts)


def project_kernel(*refs):
    pieces = refs[:-4]
    weight, gains, own_ref, other_ref = refs[-4:]
    lane = lax.broadcasted_iota(jnp.int32, (1, 2 * HD), 1)
    query_gain = gains[0:1, :]
    key_gain = gains[1:2, :]
    row = 0
    for piece in pieces:
        rows = piece.shape[0]
        for part, out_ref in ((0, own_ref), (4 * HD, other_ref)):
            out = lax.dot_general(
                piece[...],
                weight[part : part + 4 * HD, :],
                (((1,), (1,)), ((), ())),
                preferred_element_type=jnp.float32,
            )
            kv = out[:, : 2 * HD]
            q = out[:, 2 * HD :]
            key_square = jnp.where(lane < HD, kv * kv, 0.0)
            key_mean = jnp.sum(key_square, axis=-1, keepdims=True) * (1.0 / HD)
            key_scaled = kv * lax.rsqrt(key_mean + 1e-06) * key_gain
            out_ref[row : row + rows, : 2 * HD] = jnp.where(lane < HD, key_scaled, kv).astype(
                jnp.bfloat16
            )
            query_mean = jnp.sum(q * q, axis=-1, keepdims=True) * (1.0 / HD)
            out_ref[row : row + rows, 2 * HD :] = (
                q * lax.rsqrt(query_mean + 1e-06) * query_gain
            ).astype(jnp.bfloat16)
        row += rows


def projected_rows(pieces, packed_weight, gains):
    rows = sum(piece.shape[0] for piece in pieces)
    width = packed_weight.shape[1]
    out = jax.ShapeDtypeStruct((rows, 4 * HD), jnp.bfloat16)
    return pl.pallas_call(
        project_kernel,
        out_shape=(out, out),
        compiler_params=pltpu.CompilerParams(vmem_limit_bytes=40 * MIB),
        cost_estimate=pl.CostEstimate(
            flops=2 * rows * width * 512, bytes_accessed=rows * width * 2, transcendentals=0
        ),
    )(*pieces, packed_weight, gains)


def widened(kv, lane, last):
    wide = kv.astype(jnp.float32)
    front = jnp.where(lane < HD, wide, pltpu.roll(wide, HD, 1)).astype(jnp.bfloat16)
    back = jnp.where(lane < HD, wide, last).astype(jnp.bfloat16)
    pick = jnp.where(lax.broadcasted_iota(jnp.int32, (2 * HD, 2 * HD), 0) < HD, 1.0, 0.0)
    lengths = jnp.dot(
        (wide * wide).astype(jnp.bfloat16),
        pick.astype(jnp.bfloat16),
        preferred_element_type=jnp.float32,
    )
    return front, back, jnp.max(lengths, axis=0, keepdims=True)


def prepare_kernel(spots, first, second, third, text, kaug_ref, kv_ref, longest_ref):
    lane = lax.broadcasted_iota(jnp.int32, (1, 2 * HD), 1)
    start = 0
    longest = jnp.zeros((1, 2 * HD), jnp.float32)
    for source in (first, second, third, text):
        many = source.shape[0]
        kv = source[...]
        last = jnp.where((lane >= HD) & (lane < HD + 3), 1.0, 0.0)
        if source is text:
            used = lax.broadcasted_iota(jnp.int32, (many, 2 * HD), 0) < spots[pl.program_id(0)]
            last = jnp.where((lane == HD + 3) & jnp.logical_not(used), -30000.0, last)
        front, back, length = widened(kv, lane, last)
        kv_ref[start : start + many, :] = kv
        kaug_ref[start : start + many, : 2 * HD] = front
        kaug_ref[start : start + many, 2 * HD :] = back
        longest = jnp.maximum(longest, length)
        start += many
    longest_ref[...] = longest


def prepared_keys(spots, cache, text):
    branches = cache.shape[0]
    patch = cache.shape[1] // 4
    rows = 3 * patch + text.shape[1]

    def stale(step):
        return pl.BlockSpec(
            (None, patch, 2 * HD),
            lambda i, spots: (i, lax.rem(spots[2 + 2 * CHIPS] + step, 4), 0),
        )

    def each(*shape):
        return pl.BlockSpec((None, *shape), lambda i, spots: (i, 0, 0))

    return pl.pallas_call(
        prepare_kernel,
        out_shape=(
            jax.ShapeDtypeStruct((branches, rows, 4 * HD), jnp.bfloat16),
            jax.ShapeDtypeStruct((branches, rows, 2 * HD), jnp.bfloat16),
            jax.ShapeDtypeStruct((branches, 1, 2 * HD), jnp.float32),
        ),
        grid_spec=pltpu.PrefetchScalarGridSpec(
            num_scalar_prefetch=1,
            grid=(branches,),
            in_specs=[stale(1), stale(2), stale(3), each(text.shape[1], 2 * HD)],
            out_specs=(each(rows, 4 * HD), each(rows, 2 * HD), each(1, 2 * HD)),
        ),
        compiler_params=pltpu.CompilerParams(vmem_limit_bytes=40 * MIB),
        cost_estimate=pl.CostEstimate(
            flops=4 * rows * 128 * 128, bytes_accessed=rows * 2048, transcendentals=0
        ),
    )(spots, cache, cache, cache, text)


def attend_kernel(counts, branch, spots, *refs):
    pieces = refs[: sum(counts)]
    own_pieces, other_pieces = pieces[: counts[0]], pieces[counts[0] :]
    stale_kaug, stale_kv, stale_longest = refs[sum(counts) : sum(counts) + 3]
    out_ref, fresh_ref, kaug, kv_all, qaug, e_scr, total_ref, longest_ref, sems = refs[-9:]
    rows = qaug.shape[0]
    keys = kv_all.shape[0]
    stale = stale_kv.shape[1]
    lane = lax.broadcasted_iota(jnp.int32, (1, 2 * HD), 1)

    chunks = ((0, 2 * rows), (2 * rows, stale // 2), (2 * rows + stale // 2, stale // 2))
    wide_copy = pltpu.make_async_copy(stale_kaug.at[branch], kaug.at[pl.ds(2 * rows, stale), :], sems.at[0])
    kv_copy = pltpu.make_async_copy(stale_kv.at[branch], kv_all.at[pl.ds(2 * rows, stale), :], sems.at[1])

    @pl.when(pl.program_id(0) == 0)
    def _():
        wide_copy.start()
        kv_copy.start()
        start = 0
        longest = stale_longest[...]
        last = jnp.where((lane >= HD) & (lane < HD + 3), 1.0, 0.0)
        block = 0
        for source in pieces:
            many = source.shape[0]
            kv = source[:, : 2 * HD]
            front, back, length = widened(kv, lane, last)
            kv_all[start : start + many, :] = kv
            kaug[start : start + many, : 2 * HD] = front
            kaug[start : start + many, 2 * HD :] = back
            longest = jnp.maximum(longest, length)
            start += many
            for at in range(0, many, HD):
                to = pl.multiple_of(spots[2 + block] * HD, HD)
                fresh_ref[pl.ds(to, HD), :] = kv[at : at + HD, :]
                block += 1
        longest_ref[...] = longest

    own = pl.program_id(0) == 0
    scale = math.log2(math.e) / math.sqrt(HD)
    at = 0
    for mine, other in zip(own_pieces, other_pieces, strict=True):
        many = mine.shape[0]
        q = jnp.where(own, mine[:, 2 * HD :], other[:, 2 * HD :])
        scaled = q.astype(jnp.float32) * scale
        high = scaled.astype(jnp.bfloat16).astype(jnp.float32)
        left = scaled - high
        middle = left.astype(jnp.bfloat16).astype(jnp.float32)
        qaug[at : at + many, : 2 * HD] = (high + pltpu.roll(middle, HD, 1)).astype(jnp.bfloat16)
        qaug[at : at + many, 2 * HD :] = (left - middle).astype(jnp.bfloat16)
        total_ref[at : at + many, :] = jnp.broadcast_to(
            jnp.sum(scaled * scaled, axis=-1, keepdims=True), (many, 2 * HD)
        )
        at += many

    def lower(bound):
        one = bound.astype(jnp.bfloat16).astype(jnp.float32)
        rest = bound - one
        two = rest.astype(jnp.bfloat16).astype(jnp.float32)
        tail = jnp.where(lane == HD, -one, 1.0)
        tail = jnp.where(lane == HD + 1, -two, tail)
        tail = jnp.where(lane == HD + 2, two - rest, tail)
        tail = jnp.where(lane > HD + 3, 0.0, tail)
        low = qaug[:, 2 * HD :].astype(jnp.float32)
        qaug[:, 2 * HD :] = jnp.where(lane < HD, low, tail).astype(jnp.bfloat16)

    def scores(at, many):
        return lax.dot_general(
            qaug[...],
            kaug[at : at + many, :],
            (((1,), (1,)), ((), ())),
            preferred_element_type=jnp.float32,
        )

    def raise_chunk(at, many, total):
        raised = jnp.exp2(scores(at, many))
        e_scr[:, at : at + many] = raised
        for part in range(many // 128):
            total = total + raised[:, part * 128 : (part + 1) * 128]
        return total

    def keep_total(total):
        total_ref[...] = jnp.broadcast_to(jnp.sum(total, axis=-1, keepdims=True), (rows, 128))

    lower(jnp.sqrt(total_ref[...] * (longest_ref[...] * 1.02)) + 1e-3)
    total = raise_chunk(*chunks[0], jnp.zeros((rows, 128), jnp.float32))

    @pl.when(pl.program_id(0) == 0)
    def _():
        wide_copy.wait()
        kv_copy.wait()

    for chunk in chunks[1:]:
        total = raise_chunk(*chunk, total)
    keep_total(total)

    @pl.when(jnp.min(total_ref[...]) < 1e-12)
    def _():
        lower(jnp.zeros((rows, 2 * HD), jnp.float32))
        step = 2 * HD

        def best_of(j, best):
            at = pl.multiple_of(j * step, step)
            found = lax.dot_general(
                qaug[...],
                kaug[pl.ds(at, step), :],
                (((1,), (1,)), ((), ())),
                preferred_element_type=jnp.float32,
            )
            return jnp.maximum(best, found)

        best = lax.fori_loop(
            0, keys // step, best_of, jnp.full((rows, step), -3e38, jnp.float32)
        )
        best = jnp.max(best, axis=-1, keepdims=True)
        lower(jnp.broadcast_to(best, (rows, 2 * HD)))

        def raise_part(j, total):
            at = pl.multiple_of(j * step, step)
            raised = jnp.exp2(
                lax.dot_general(
                    qaug[...],
                    kaug[pl.ds(at, step), :],
                    (((1,), (1,)), ((), ())),
                    preferred_element_type=jnp.float32,
                )
            )
            e_scr[:, pl.ds(at, step)] = raised
            return total + raised

        keep_total(
            lax.fori_loop(0, keys // step, raise_part, jnp.zeros((rows, step), jnp.float32))
        )

    share = 1.0 / total_ref[...]
    def weigh(j, sums):
        at = pl.multiple_of(j * 2816, 2816)
        probs = e_scr[:, pl.ds(at, 2816)] * jnp.tile(share, (1, 2816 // 128))
        return sums + jnp.dot(
            probs.astype(jnp.bfloat16),
            kv_all[pl.ds(at, 2816), :],
            preferred_element_type=jnp.float32,
        )

    sums = lax.fori_loop(0, keys // 2816, weigh, jnp.zeros((rows, 2 * HD), jnp.float32))
    for block in range(CHIPS):
        top = sums[block * HD : block * HD + HD // 2, :]
        bottom = sums[block * HD + HD // 2 : (block + 1) * HD, :]
        joined = jnp.where(lane < HD, pltpu.roll(top, HD, 1), bottom)
        out_ref[spots[2 + pl.program_id(0) * CHIPS + block]] = joined.astype(jnp.bfloat16)


def attended_rows(spots, branch, own_pieces, other_pieces, prepared, earlier):
    pieces = (*own_pieces, *other_pieces)
    rows = sum(piece.shape[0] for piece in own_pieces)
    patch = 2 * rows
    keys = prepared[1].shape[1] + patch

    def whole(part):
        return pl.BlockSpec(part.shape, lambda i, spots: (0, 0))

    out_shape = (
        jax.ShapeDtypeStruct((2 * CHIPS, HD, 2 * HD), jnp.bfloat16),
        jax.ShapeDtypeStruct((2, patch, 2 * HD), jnp.bfloat16),
    )
    out_specs = (
        pl.BlockSpec((2 * CHIPS, HD // 2, 2 * HD), lambda i, spots: (0, branch, 0)),
        pl.BlockSpec((None, patch, 2 * HD), lambda i, spots: (branch, 0, 0)),
    )
    anywhere = pl.BlockSpec(memory_space=pl.ANY)
    return pl.pallas_call(
        functools.partial(attend_kernel, (len(own_pieces), len(other_pieces)), branch),
        out_shape=out_shape,
        grid_spec=pltpu.PrefetchScalarGridSpec(
            num_scalar_prefetch=1,
            grid=(2,),
            in_specs=[whole(part) for part in pieces]
            + [anywhere, anywhere]
            + [pl.BlockSpec((None, 1, 2 * HD), lambda i, spots: (branch, 0, 0))]
            + [anywhere] * len(earlier),
            out_specs=out_specs,
            scratch_shapes=[
                pltpu.VMEM((keys, 4 * HD), jnp.bfloat16),
                pltpu.VMEM((keys, 2 * HD), jnp.bfloat16),
                pltpu.VMEM((rows, 4 * HD), jnp.bfloat16),
                pltpu.VMEM((rows, keys), jnp.float32),
                pltpu.VMEM((rows, 2 * HD), jnp.float32),
                pltpu.VMEM((1, 2 * HD), jnp.float32),
                pltpu.SemaphoreType.DMA((2,)),
            ],
        ),
        input_output_aliases={1 + len(pieces) + 3 + i: i for i in range(len(earlier))},
        compiler_params=pltpu.CompilerParams(vmem_limit_bytes=48 * MIB),
        cost_estimate=pl.CostEstimate(
            flops=4 * patch * keys * 256, bytes_accessed=8 * MIB, transcendentals=0
        ),
    )(spots, *pieces, *prepared, *earlier)


def finish_kernel(heads, weight, entering, gate, out_ref, lhs, total):
    step = pl.program_id(0)
    rows = entering.shape[1]
    lane = lax.broadcasted_iota(jnp.int32, (1, 2 * HD), 1)

    @pl.when(step == 0)
    def _():
        for pair in range(CHIPS):
            low = heads[2 * pair].astype(jnp.float32)
            high = heads[2 * pair + 1].astype(jnp.float32)
            top = jnp.where(lane < HD, low, pltpu.roll(high, HD, 1)).astype(jnp.bfloat16)
            bottom = jnp.where(lane < HD, pltpu.roll(low, HD, 1), high).astype(jnp.bfloat16)
            at = (pair % SIDE) * 2 * HD
            for branch in range(2):
                from_row = branch * rows // 2
                to = branch * rows
                here = slice(at, at + 2 * HD)
                part = slice(from_row, from_row + rows // 2)
                lhs[pair // SIDE, to : to + rows // 2, here] = top[part]
                lhs[pair // SIDE, to + rows // 2 : to + rows, here] = bottom[part]

    part = jnp.dot(lhs[step], weight[...], preferred_element_type=jnp.float32)

    @pl.when(step == 0)
    def _():
        total[...] = part

    @pl.when(step > 0)
    def _():
        total[...] += part

    @pl.when(step == SIDE - 1)
    def _():
        for branch in range(2):
            sums = total[branch * rows : (branch + 1) * rows, :]
            out_ref[branch] = (entering[branch].astype(jnp.float32) + gate[2:3, :] * sums).astype(
                jnp.bfloat16
            )


def finished_rows(heads, weight, entering, mod_rows):
    rows, width = entering.shape[1:]
    depth = weight.shape[0] // SIDE
    return pl.pallas_call(
        finish_kernel,
        out_shape=jax.ShapeDtypeStruct(entering.shape, jnp.bfloat16),
        grid=(SIDE,),
        in_specs=[
            pl.BlockSpec(heads.shape, lambda i: (0, 0, 0)),
            pl.BlockSpec((depth, width), lambda i: (i, 0)),
            pl.BlockSpec(entering.shape, lambda i: (0, 0, 0)),
            pl.BlockSpec((3, width), lambda i: (0, 0)),
        ],
        out_specs=pl.BlockSpec(entering.shape, lambda i: (0, 0, 0)),
        scratch_shapes=[
            pltpu.VMEM((SIDE, 2 * rows, depth), jnp.bfloat16),
            pltpu.VMEM((2 * rows, width), jnp.float32),
        ],
        compiler_params=pltpu.CompilerParams(vmem_limit_bytes=24 * MIB),
        cost_estimate=pl.CostEstimate(
            flops=4 * rows * width * weight.shape[0],
            bytes_accessed=weight.shape[0] * width * 2,
            transcendentals=0,
        ),
    )(heads, weight, entering, mod_rows)


def local(
    patch_in,
    modulation,
    qkv_weight,
    qk_gain,
    out_weight,
    kv_cache,
    text_kv,
    patch_offsets,
    step_index,
    text_count,
):
    entering = patch_in[0]
    mod_rows = modulation[0]
    normed = normed_rows(entering, mod_rows)

    line = [normed] + [along(normed, 0, step) for step in STEPS[1:]]
    line_0, line_1 = split_rows(line)

    patch_offsets, step_index, text_count = after(
        (patch_offsets, step_index, text_count), normed
    )
    section_index = lax.axis_index("section")
    place = lax.axis_index("seq")
    core = place % 2
    x = (place // 2) % SIDE
    z = place // (2 * SIDE)
    patch_total = patch_offsets.shape[0]
    patch_number = (step_index[0] - section_index) % patch_total
    offset = jnp.sum(
        jnp.where(jnp.arange(patch_total, dtype=jnp.int32) == patch_number, patch_offsets, 0)
    )
    steps = jnp.array(STEPS, jnp.int32)
    outer = jnp.repeat(steps, SIDE)
    inner = jnp.tile(steps, SIDE)

    def chips_of(side):
        down = jnp.where(side == 0, outer, inner)
        across = jnp.where(side == 0, inner, outer)
        return ((z - down) % SIDE) * SIDE + (x - across) % SIDE

    fresh_places = jnp.concatenate(
        [chips_of(core) * 2 + core, chips_of(1 - core) * 2 + (1 - core)]
    )
    patch_rows = kv_cache.shape[2] // patch_total
    spots = jnp.concatenate([text_count, fresh_places, (offset // patch_rows)[None]])
    spots = spots.astype(jnp.int32)
    line_0, spots = lax.optimization_barrier((line_0, spots))
    left = along(line_0, 1, 1)
    right = along(line_0, 1, -1)
    cache, text, qkv_weight, qk_gain = after((kv_cache[0], text_kv[0], qkv_weight, qk_gain), line_0)
    weight = qkv_weight[0].T
    packed_weight = packed_rows(weight, swapped(weight))
    gains = jnp.pad(qk_gain[0], ((0, 0), (0, HD)), constant_values=1.0)
    prepared = prepared_keys(spots, cache, text)
    left, right, prepared, packed_weight, gains = lax.optimization_barrier(
        (left, right, prepared, packed_weight, gains)
    )

    def project(pieces):
        own, other = projected_rows(pieces, packed_weight, gains)
        return own, swapped(other)

    half = line_0.shape[0] // 2
    far_low = along(left[:half], 1, 1)
    far_high = along(right[half:], 1, -1)
    own_near, other_near = project([line_0, left, right])
    far_low, far_high, line_1 = lax.optimization_barrier((far_low, far_high, line_1))
    left_1 = along(line_1, 1, 1)
    right_1 = along(line_1, 1, -1)
    far_1 = along(line_1, 1, 2)
    own_far, other_far = project([far_low, far_high])
    first = attended_rows(
        spots, 0, (own_near, own_far), (other_near, other_far), prepared, ()
    )
    left_1, right_1, far_1, first = lax.optimization_barrier((left_1, right_1, far_1, first))
    own_all, other_all = project([line_1, left_1, right_1, far_1])
    attended, fresh = attended_rows(spots, 1, (own_all,), (other_all,), prepared, first)

    heads = lax.all_to_all(attended, "seq", split_axis=0, concat_axis=0, tiled=True)
    done = finished_rows(heads, out_weight[0], entering, mod_rows)
    count = lax.axis_size("section")
    moved = lax.ppermute(done, "section", [(i, (i + 1) % count) for i in range(count)])
    return (moved[None], fresh[None])


def solution(mesh):
    in_specs = (
        P("section", None, "seq", None),
        P("section", None, None),
        P("section", None, "seq"),
        P("section", None, None),
        P("section", None, None),
        P("section", None, None, "seq"),
        P("section", None, None, "seq"),
        P(),
        P(),
        P(),
    )
    out_specs = (P("section", None, "seq", None), P("section", None, None, "seq"))
    return jax.shard_map(local, mesh=mesh, in_specs=in_specs, out_specs=out_specs, check_vma=False)
```

time: 458 us -> 341 us (0.74)
  Pallas kernels: 0 us -> 249 us
  matrix products: 141 us -> 0 us
  waiting for transfers between devices: 132 us -> 32.1 us
  other arithmetic: 72.1 us -> 0.8 us
  local copies, waits for them, and re-layouts: 70.7 us -> 9.85 us
  starting transfers between devices: 6.6 us -> 26.5 us
  between operations: 16.9 us -> 4.21 us
    pallas_call x0 -> x10, Pallas kernels: none -> 249 us  [the longest x2 232 us: attended_rows(): pl.pallas_call(functools.partial(attend_kernel, (len(own_pieces), len(oth...]
    dot_general x10 -> x0, matrix products: 141 us -> none  [the longest x4 64.8 us: block_attend(): jnp.einsum('bhqk,bkhd->bqhd', probs, value_vecs, preferred_element_type=j...]
    all_gather x1 -> x0, waiting for transfers between devices: 106 us -> none  [local(): lax.all_gather(qkv_weight[0], 'seq', axis=1, tiled=True)]
    reduce_sum x7 -> x0, other arithmetic: 64.7 us -> none  [the longest x4 61.3 us: block_attend(): totals = jnp.sum(raised, axis=-1, keepdims=True)]
    convert_element_type x1 -> x0, local copies, waits for them, and re-layouts: 26.7 us -> none  [normalize_heads(): jnp.stack([queries, keys_new, values_new], axis=3).astype(jnp.bfloat16)]
    ppermute x1 -> x15, starting transfers between devices: 1.27 us -> 26.5 us  [the longest x10 15.1 us: along(): return lax.ppermute(value, 'seq', pairs_of(phase, step))]
    ppermute x1 -> x15, waiting for transfers between devices: 13.9 us -> 32.1 us  [the longest x1 15.2 us: local(): lax.ppermute(done, 'section', [(i, (i + 1) % count) for i in range(count)])]
    all_to_all x1 -> x0, waiting for transfers between devices: 12.3 us -> none  [local(): lax.all_to_all(packed_local, 'seq', split_axis=2, concat_axis=1, tiled=True)]
  transfers between devices with their start and end apart: 3 -> 15, of which waited for: 3 -> 7; matrix products, arithmetic and copies ran while one was open for 3% -> 0% of each run, Pallas kernels for 0% -> 37%
where the time goes in v1:
time: 341 us
  Pallas kernels  249 us (73%)
  waiting for transfers between devices  32.1 us (9%)
  starting transfers between devices  26.5 us (8%)
  blocking collectives  18.7 us (5%)
  local copies, waits for them, and re-layouts  9.85 us (3%)
  between operations  4.21 us (1%)
    pallas_call x2, Pallas kernels, attended_rows(): pl.pallas_call(functools.partial(attend_kernel, (len(own_pieces), len(oth...  232 us
    all_to_all x1, blocking collectives, local(): lax.all_to_all(attended, 'seq', split_axis=0, concat_axis=0, tiled=True)  18.7 us
    ppermute x1, waiting for transfers between devices, local(): lax.ppermute(done, 'section', [(i, (i + 1) % count) for i in range(count)])  15.2 us
    ppermute x10, starting transfers between devices, along(): return lax.ppermute(value, 'seq', pairs_of(phase, step))  15.1 us
    ppermute x10, waiting for transfers between devices, along(): return lax.ppermute(value, 'seq', pairs_of(phase, step))  15.1 us
    ppermute x4, starting transfers between devices, swapped(): return lax.ppermute(value, 'seq', [(i, i ^ 1) for i in range(2 * CHIPS)])  9.94 us
    unnamed x34, local copies, waits for them, and re-layouts  9.43 us
    pallas_call x3, Pallas kernels, projected_rows(): pl.pallas_call(project_kernel, out_shape=(out, out), compiler_params=pltp...  8.61 us
  transfers between devices with their start and end apart: 15, of which 7 were waited for; matrix products, arithmetic and copies ran while one was open for 0% of the time, Pallas kernels for 37%

profile of v1, /device:TPU:1, one launch (start us, length us, event | category | flops | bytes accessed | tf_op | source)
XLA Modules:
  0.0 340.9 jit_solution(10301589958769771918)
XLA Ops:
  3.0 4.5 %collective-permute-start.2 = (bf16[128,2432]{1,0:T(8,128)(2,1)S(1)}, bf16[128,2432]{1,0:T(8,128)(2,1)S(1)}, u32[]{:S(2)}, u32[]{:S(2)}) collective-permute-start(bf16[128,2432]{1,0:T(8,128)(2,1)S(1)} %shard_map.122.refs_0_), channel_id=1, source_target_pairs={{0,4},{1,17},{2,6},{3,19},{4,0},{5,21},{6,2},{7,23},{8,12},{9,25},... | collective-permute-start | bytes 1867784 | tf_op jit(solution)/shard_map/ppermute | solution.py:32
  13.5 2.0 collective-permute-done.2.refs_3_
  15.5 7.3 %collective-permute-done.1.refs_2_ = bf16[128,2432]{1,0:T(8,128)(2,1)S(1)} collective-permute-done((bf16[128,2432]{1,0:T(8,128)(2,1)S(1)}, bf16[128,2432]{1,0:T(8,128)(2,1)S(1)}, u32[]{:S(2)}, u32[]{:S(2)}) %collective-permute-start.1) | collective-permute-done | bytes 622624 | tf_op jit(solution)/shard_map/ppermute | solution.py:32
  23.9 2.4 collective-permute-start.4
  26.3 2.1 collective-permute-start.5
  28.4 2.2 copy-done
  30.6 3.3 shard_map.124
  33.9 2.8 copy-done.5
  36.6 1.8 copy-done.6
  38.6 1.9 collective-permute-done.4.refs_2_
  40.5 3.3 collective-permute-done.3.refs_1_
  43.9 2.7 collective-permute-start.7
  46.6 3.7 %shard_map.126 = (bf16[768,256]{1,0:T(8,128)(2,1)S(1)}, bf16[768,256]{1,0:T(8,128)(2,1)S(1)}) custom-call(bf16[256,2432]{1,0:T(8,128)(2,1)} %get-tuple-element.46.refs_0_, bf16[256,2432]{1,0:T(8,128)(2,1)S(1)} %collective-permute-done.3.refs_1_, bf16[256,2432]{1,0:T(8,128)(2,1)S(1)} %collective-permute-done.4.refs_2_, ...), custom_call_target="tpu_custom_call" | custom-call | flops 1912602624 | bytes 3735552 | tf_op jit(solution)/shard_map/pallas_call | solution.py:134
  50.3 3.6 %collective-permute-start.11 = (bf16[768,256]{1,0:T(8,128)(2,1)S(1)}, bf16[768,256]{1,0:T(8,128)(2,1)S(1)}, u32[]{:S(2)}, u32[]{:S(2)}) collective-permute-start(bf16[768,256]{1,0:T(8,128)(2,1)S(1)} %get-tuple-element.64), channel_id=1, source_target_pairs={{0,1},{1,0},{2,3},{3,2},{4,5},{5,4},{6,7},{7,6},{8,9},{9,8},{10,11... | collective-permute-start | bytes 1179656 | tf_op jit(solution)/shard_map/ppermute | solution.py:36
  54.5 1.8 shard_map.127
  56.4 3.9 %collective-permute-start.12 = (bf16[256,256]{1,0:T(8,128)(2,1)S(1)}, bf16[256,256]{1,0:T(8,128)(2,1)S(1)}, u32[]{:S(2)}, u32[]{:S(2)}) collective-permute-start(bf16[256,256]{1,0:T(8,128)(2,1)S(1)} %get-tuple-element.65), channel_id=1, source_target_pairs={{0,1},{1,0},{2,3},{3,2},{4,5},{5,4},{6,7},{7,6},{8,9},{9,8},{10,11... | collective-permute-start | bytes 393224 | tf_op jit(solution)/shard_map/ppermute | solution.py:36
  60.2 2.6 collective-permute-start.10
  64.3 115.5 %shard_map.128 = (bf16[32,64,128]{2,1,0:T(8,128)(2,1)S(1)}, bf16[2,2048,128]{2,1,0:T(8,128)(2,1)}) custom-call(s32[35]{0:T(128)S(1)} %pad_add_fusion.spots, bf16[768,256]{1,0:T(8,128)(2,1)S(1)} %get-tuple-element.60.refs_0_, bf16[256,256]{1,0:T(8,128)(2,1)S(1)} %get-tuple-element.63.refs_1_, bf16[768,256]{1,0:T(8,128)(2,1)S(1)} %collective-permute-done.11.refs_2_, ...), custom_call_target="tpu_custom_call" | custom-call | flops 17716740096 | bytes 8388608 | tf_op jit(solution)/shard_map/pallas_call | solution.py:380
  179.9 3.1 shard_map.129
  183.4 1.8 collective-permute-done.13.refs_1_
  185.2 116.6 %shard_map.130 = (bf16[32,64,128]{2,1,0:T(8,128)(2,1)S(1)}, bf16[2,2048,128]{2,1,0:T(8,128)(2,1)}) custom-call(s32[35]{0:T(128)S(1)} %pad_add_fusion.spots, bf16[1024,256]{1,0:T(8,128)(2,1)S(1)} %get-tuple-element.74.refs_0_, bf16[1024,256]{1,0:T(8,128)(2,1)S(1)} %collective-permute-done.13.refs_1_, ...), custom_call_target="tpu_custom_call", output_to_operand_aliasing={{0}: (6, {}), {1}: (7, {})} | custom-call | flops 17716740096 | bytes 8388608 | tf_op jit(solution)/shard_map/pallas_call | solution.py:380
  301.8 18.7 %all_to_all.5.heads = bf16[32,64,128]{2,1,0:T(8,128)(2,1)S(1)} all-to-all(bf16[32,64,128]{2,1,0:T(8,128)(2,1)S(1)} %get-tuple-element.78), channel_id=1, replica_groups=mesh['section'=4,'seq'=32] {'seq'}, dimensions={0} | all-to-all | bytes 1048576 | tf_op jit(solution)/shard_map/all_to_all | solution.py:555
  320.5 2.9 shard_map.131
  324.9 15.2 %collective-permute-done.14 = bf16[2,64,2432]{2,1,0:T(8,128)(2,1)S(1)} collective-permute-done((bf16[2,64,2432]{2,1,0:T(8,128)(2,1)S(1)}, bf16[2,64,2432]{2,1,0:T(8,128)(2,1)S(1)}, u32[]{:S(2)}, u32[]{:S(2)}) %collective-permute-start.14) | collective-permute-done | bytes 622624 | tf_op jit(solution)/shard_map/ppermute | solution.py:558
  (63 shorter events, 11.3 us)
Async XLA Ops:
  0.6 11.6 %copy-start.9 = (s32[4]{0:T(128)S(1)}, s32[4]{0:T(128)}, u32[]{:S(2)}) copy-start(s32[4]{0:T(128)} %constant.99.clone) | copy-start | bytes 52
  0.6 12.7 %copy-start.11 = (s32[2]{0:T(128)S(1)}, s32[2]{0:T(128)}, u32[]{:S(2)}) copy-start(s32[2]{0:T(128)} %param.20) | copy-start | bytes 28
  3.0 12.5 %collective-permute-start.2 = (bf16[128,2432]{1,0:T(8,128)(2,1)S(1)}, bf16[128,2432]{1,0:T(8,128)(2,1)S(1)}, u32[]{:S(2)}, u32[]{:S(2)}) collective-permute-start(bf16[128,2432]{1,0:T(8,128)(2,1)S(1)} %shard_map.122.refs_0_), channel_id=1, source_target_pairs={{0,4},{1,17},{2,6},{3,19},{4,0},{5,21},{6,2},{7,23},{8,12},{9,25},... | collective-permute-start | bytes 1867784 | tf_op jit(solution)/shard_map/ppermute | solution.py:32
  7.5 15.2 %collective-permute-start.1 = (bf16[128,2432]{1,0:T(8,128)(2,1)S(1)}, bf16[128,2432]{1,0:T(8,128)(2,1)S(1)}, u32[]{:S(2)}, u32[]{:S(2)}) collective-permute-start(bf16[128,2432]{1,0:T(8,128)(2,1)S(1)} %shard_map.122.refs_0_), channel_id=1, source_target_pairs={{0,6},{1,25},{2,0},{3,27},{4,2},{5,29},{6,4},{7,31},{8,14},{9,1},{... | collective-permute-start | bytes 1867784 | tf_op jit(solution)/shard_map/ppermute | solution.py:32
  7.9 14.8 %collective-permute-start = (bf16[128,2432]{1,0:T(8,128)(2,1)S(1)}, bf16[128,2432]{1,0:T(8,128)(2,1)S(1)}, u32[]{:S(2)}, u32[]{:S(2)}) collective-permute-start(bf16[128,2432]{1,0:T(8,128)(2,1)S(1)} %shard_map.122.refs_0_), channel_id=1, source_target_pairs={{0,2},{1,9},{2,4},{3,11},{4,6},{5,13},{6,0},{7,15},{8,10},{9,17},{... | collective-permute-start | bytes 1867784 | tf_op jit(solution)/shard_map/ppermute | solution.py:32
  13.5 12.8 %copy-start.3 = (bf16[1,2432,192]{1,2,0:T(8,128)(2,1)S(1)}, bf16[1,2432,192]{1,2,0:T(8,128)(2,1)}, u32[]{:S(2)}) copy-start(bf16[1,2432,192]{1,2,0:T(8,128)(2,1)} %param.13) | copy-start | bytes 2801668
  13.5 14.9 %copy-start.10 = (f32[1,2,64]{2,1,0:T(2,128)S(1)}, f32[1,2,64]{2,1,0:T(2,128)}, u32[]{:S(2)}) copy-start(f32[1,2,64]{2,1,0:T(2,128)} %param.14) | copy-start | bytes 1540
  13.5 14.9 %copy-start.4 = (bf16[1,2,256,128]{3,2,1,0:T(8,128)(2,1)S(1)}, bf16[1,2,256,128]{3,2,1,0:T(8,128)(2,1)}, u32[]{:S(2)}) copy-start(bf16[1,2,256,128]{3,2,1,0:T(8,128)(2,1)} %param.17) | copy-start | bytes 393220
  23.9 16.5 %collective-permute-start.4 = (bf16[256,2432]{1,0:T(8,128)(2,1)}, bf16[256,2432]{1,0:T(8,128)(2,1)S(1)}, u32[]{:S(2)}, u32[]{:S(2)}) collective-permute-start(bf16[256,2432]{1,0:T(8,128)(2,1)} %get-tuple-element.46.refs_0_), channel_id=1, source_target_pairs={{0,24},{1,7},{2,26},{3,1},{4,28},{5,3},{6,30},{7,5},{8,0},{9,15},{... | collective-permute-start | bytes 3735560 | tf_op jit(solution)/shard_map/ppermute | solution.py:32
  26.3 17.5 %collective-permute-start.3 = (bf16[256,2432]{1,0:T(8,128)(2,1)}, bf16[256,2432]{1,0:T(8,128)(2,1)S(1)}, u32[]{:S(2)}, u32[]{:S(2)}) collective-permute-start(bf16[256,2432]{1,0:T(8,128)(2,1)} %get-tuple-element.46.refs_0_), channel_id=1, source_target_pairs={{0,8},{1,3},{2,10},{3,5},{4,12},{5,7},{6,14},{7,1},{8,16},{9,11},{... | collective-permute-start | bytes 3735560 | tf_op jit(solution)/shard_map/ppermute | solution.py:32
  26.3 12.1 %collective-permute-start.5 = (bf16[192,2432]{1,0:T(8,128)(2,1)S(1)}, bf16[192,2432]{1,0:T(8,128)(2,1)S(1)}, u32[]{:S(2)}, u32[]{:S(2)}) collective-permute-start(bf16[192,2432]{1,0:T(8,128)(2,1)S(1)} %bitcast.24), channel_id=1, source_target_pairs={{0,1},{1,0},{2,3},{3,2},{4,5},{5,4},{6,7},{7,6},{8,9},{9,8},{10,11... | collective-permute-start | bytes 2801672 | tf_op jit(solution)/shard_map/ppermute | solution.py:36
  43.9 10.7 %collective-permute-start.6 = (bf16[128,2432]{1,0:T(8,128)(2,1)S(1)}, bf16[128,2432]{1,0:T(8,128)(2,1)S(1)}, u32[]{:S(2)}, u32[]{:S(2)}) collective-permute-start(bf16[128,2432]{1,0:T(8,128)(2,1)S(1)} %slice.6), channel_id=1, source_target_pairs={{0,8},{1,3},{2,10},{3,5},{4,12},{5,7},{6,14},{7,1},{8,16},{9,11},{... | collective-permute-start | bytes 1867784 | tf_op jit(solution)/shard_map/ppermute | solution.py:32
  43.9 10.6 %collective-permute-start.7 = (bf16[128,2432]{1,0:T(8,128)(2,1)S(1)}, bf16[128,2432]{1,0:T(8,128)(2,1)S(1)}, u32[]{:S(2)}, u32[]{:S(2)}) collective-permute-start(bf16[128,2432]{1,0:T(8,128)(2,1)S(1)} %slice.7), channel_id=1, source_target_pairs={{0,24},{1,7},{2,26},{3,1},{4,28},{5,3},{6,30},{7,5},{8,0},{9,15},{... | collective-permute-start | bytes 1867784 | tf_op jit(solution)/shard_map/ppermute | solution.py:32
  50.3 14.0 %collective-permute-start.11 = (bf16[768,256]{1,0:T(8,128)(2,1)S(1)}, bf16[768,256]{1,0:T(8,128)(2,1)S(1)}, u32[]{:S(2)}, u32[]{:S(2)}) collective-permute-start(bf16[768,256]{1,0:T(8,128)(2,1)S(1)} %get-tuple-element.64), channel_id=1, source_target_pairs={{0,1},{1,0},{2,3},{3,2},{4,5},{5,4},{6,7},{7,6},{8,9},{9,8},{10,11... | collective-permute-start | bytes 1179656 | tf_op jit(solution)/shard_map/ppermute | solution.py:36
  56.4 8.0 %collective-permute-start.12 = (bf16[256,256]{1,0:T(8,128)(2,1)S(1)}, bf16[256,256]{1,0:T(8,128)(2,1)S(1)}, u32[]{:S(2)}, u32[]{:S(2)}) collective-permute-start(bf16[256,256]{1,0:T(8,128)(2,1)S(1)} %get-tuple-element.65), channel_id=1, source_target_pairs={{0,1},{1,0},{2,3},{3,2},{4,5},{5,4},{6,7},{7,6},{8,9},{9,8},{10,11... | collective-permute-start | bytes 393224 | tf_op jit(solution)/shard_map/ppermute | solution.py:36
  60.2 119.6 %collective-permute-start.10 = (bf16[256,2432]{1,0:T(8,128)(2,1)S(1)}, bf16[256,2432]{1,0:T(8,128)(2,1)S(1)}, u32[]{:S(2)}, u32[]{:S(2)}) collective-permute-start(bf16[256,2432]{1,0:T(8,128)(2,1)S(1)} %get-tuple-element.57.refs_0_), channel_id=1, source_target_pairs={{0,16},{1,5},{2,18},{3,7},{4,20},{5,1},{6,22},{7,3},{8,24},{9,13},... | collective-permute-start | bytes 3735560 | tf_op jit(solution)/shard_map/ppermute | solution.py:32
  62.9 117.0 %collective-permute-start.9 = (bf16[256,2432]{1,0:T(8,128)(2,1)S(1)}, bf16[256,2432]{1,0:T(8,128)(2,1)S(1)}, u32[]{:S(2)}, u32[]{:S(2)}) collective-permute-start(bf16[256,2432]{1,0:T(8,128)(2,1)S(1)} %get-tuple-element.57.refs_0_), channel_id=1, source_target_pairs={{0,24},{1,7},{2,26},{3,1},{4,28},{5,3},{6,30},{7,5},{8,0},{9,15},{... | collective-permute-start | bytes 3735560 | tf_op jit(solution)/shard_map/ppermute | solution.py:32
  63.8 116.1 %collective-permute-start.8 = (bf16[256,2432]{1,0:T(8,128)(2,1)S(1)}, bf16[256,2432]{1,0:T(8,128)(2,1)S(1)}, u32[]{:S(2)}, u32[]{:S(2)}) collective-permute-start(bf16[256,2432]{1,0:T(8,128)(2,1)S(1)} %get-tuple-element.57.refs_0_), channel_id=1, source_target_pairs={{0,8},{1,3},{2,10},{3,5},{4,12},{5,7},{6,14},{7,1},{8,16},{9,11},{... | collective-permute-start | bytes 3735560 | tf_op jit(solution)/shard_map/ppermute | solution.py:32
  183.0 2.2 collective-permute-start.13
  185.2 135.3 %slice-start = ((s8[9961472]{0:T(1024)(128)(4,1)}), s8[4194304]{0:T(1024)(128)(4,1)S(1)}, s32[]{:S(2)}) async-start(s8[9961472]{0:T(1024)(128)(4,1)} %bitcast.19), calls=%async_computation.1 | async-start | bytes 8388608
  185.2 135.3 %slice-start.1 = ((s8[9961472]{0:T(1024)(128)(4,1)}), s8[4194304]{0:T(1024)(128)(4,1)S(1)}, s32[]{:S(2)}) async-start(s8[9961472]{0:T(1024)(128)(4,1)} %bitcast.19), calls=%async_computation.2 | async-start | bytes 8388608
  185.2 135.3 %slice-start.2 = ((s8[9961472]{0:T(1024)(128)(4,1)}), s8[1572864]{0:T(1024)(128)(4,1)S(1)}, s32[]{:S(2)}) async-start(s8[9961472]{0:T(1024)(128)(4,1)} %bitcast.19), calls=%async_computation.3 | async-start | bytes 3145728
  301.8 18.7 %copy-start.2 = (bf16[1,2,64,2432]{3,2,1,0:T(8,128)(2,1)S(1)}, bf16[1,2,64,2432]{3,2,1,0:T(8,128)(2,1)}, u32[]{:S(2)}) copy-start(bf16[1,2,64,2432]{3,2,1,0:T(8,128)(2,1)} %param.11) | copy-start | bytes 1867780
  323.5 16.6 %collective-permute-start.14 = (bf16[2,64,2432]{2,1,0:T(8,128)(2,1)S(1)}, bf16[2,64,2432]{2,1,0:T(8,128)(2,1)S(1)}, u32[]{:S(2)}, u32[]{:S(2)}) collective-permute-start(bf16[2,64,2432]{2,1,0:T(8,128)(2,1)S(1)} %shard_map.131), channel_id=1, source_target_pairs={{0,32},{32,64},{64,96},{96,0},{1,33},{33,65},{65,97},{97,1},{2,34}... | collective-permute-start | bytes 1867784 | tf_op jit(solution)/shard_map/ppermute | solution.py:558
  (7 other events, 31.9 us)

commit v2 on v1

--- a/solution.py
+++ b/solution.py
@@ -41,24 +41,25 @@
 
 
 def norm_kernel(x_ref, mod_ref, out_ref):
-    shift = mod_ref[0:1, :]
-    scale = 1.0 + mod_ref[1:2, :]
-    rows = x_ref.shape[1]
-    for branch in range(2):
-        values = x_ref[branch].astype(jnp.float32)
-        center = jnp.mean(values, axis=-1, keepdims=True)
-        moved = values - center
-        spread = jnp.mean(moved * moved, axis=-1, keepdims=True)
-        out_ref[branch * rows : (branch + 1) * rows, :] = (
-            moved * lax.rsqrt(spread + 1e-06) * scale + shift
-        ).astype(jnp.bfloat16)
-
-
-def normed_rows(entering, mod_rows):
+    values = x_ref[...].astype(jnp.float32)
+    center = jnp.mean(values, axis=-1, keepdims=True)
+    moved = values - center
+    spread = jnp.mean(moved * moved, axis=-1, keepdims=True)
+    scaled = moved * lax.rsqrt(spread + 1e-06) * (1.0 + mod_ref[1:2, :])
+    out_ref[...] = (scaled + mod_ref[0:1, :]).astype(jnp.bfloat16)
+
+
+def normed_rows(entering, branch, mod_rows):
     rows, width = entering.shape[1:]
     return pl.pallas_call(
         norm_kernel,
-        out_shape=jax.ShapeDtypeStruct((2 * rows, width), jnp.bfloat16),
+        out_shape=jax.ShapeDtypeStruct((rows, width), jnp.bfloat16),
+        grid=(1,),
+        in_specs=[
+            pl.BlockSpec((None, rows, width), lambda i: (branch, 0, 0)),
+            pl.BlockSpec(mod_rows.shape, lambda i: (0, 0)),
+        ],
+        out_specs=pl.BlockSpec((rows, width), lambda i: (0, 0)),
         compiler_params=pltpu.CompilerParams(vmem_limit_bytes=16 * MIB),
     )(entering, mod_rows)
 
@@ -78,21 +79,21 @@
     )(own, other)
 
 
-def split_kernel(*refs):
+def join_kernel(*refs):
     parts, outs = refs[:-2], refs[-2:]
-    rows = parts[0].shape[0] // 2
-    for branch, out_ref in enumerate(outs):
-        for i, part in enumerate(parts):
-            out_ref[i * rows : (i + 1) * rows, :] = part[branch * rows : (branch + 1) * rows, :]
-
-
-def split_rows(parts):
+    rows = parts[0].shape[0]
+    for i, part in enumerate(parts):
+        at = i % 2 * rows
+        outs[i // 2][at : at + rows, :] = part[...]
+
+
+def joined_rows(parts):
     rows, width = parts[0].shape
-    out = jax.ShapeDtypeStruct((rows // 2 * len(parts), width), parts[0].dtype)
-    return pl.pallas_call(
-        split_kernel,
+    out = jax.ShapeDtypeStruct((2 * rows, width), parts[0].dtype)
+    return pl.pallas_call(
+        join_kernel,
         out_shape=(out, out),
-        compiler_params=pltpu.CompilerParams(vmem_limit_bytes=24 * MIB),
+        compiler_params=pltpu.CompilerParams(vmem_limit_bytes=16 * MIB),
     )(*parts)
 
 
@@ -201,7 +202,7 @@
             in_specs=[stale(1), stale(2), stale(3), each(text.shape[1], 2 * HD)],
             out_specs=(each(rows, 4 * HD), each(rows, 2 * HD), each(1, 2 * HD)),
         ),
-        compiler_params=pltpu.CompilerParams(vmem_limit_bytes=40 * MIB),
+        compiler_params=pltpu.CompilerParams(vmem_limit_bytes=60 * MIB),
         cost_estimate=pl.CostEstimate(
             flops=4 * rows * 128 * 128, bytes_accessed=rows * 2048, transcendentals=0
         ),
@@ -487,13 +488,13 @@
 ):
     entering = patch_in[0]
     mod_rows = modulation[0]
-    normed = normed_rows(entering, mod_rows)
-
-    line = [normed] + [along(normed, 0, step) for step in STEPS[1:]]
-    line_0, line_1 = split_rows(line)
+    def first_round(rows):
+        return [rows] + [along(rows, 0, step) for step in STEPS[1:]]
+
+    line = first_round(normed_rows(entering, 0, mod_rows))
 
     patch_offsets, step_index, text_count = after(
-        (patch_offsets, step_index, text_count), normed
+        (patch_offsets, step_index, text_count), line[0]
     )
     section_index = lax.axis_index("section")
     place = lax.axis_index("seq")
@@ -520,27 +521,30 @@
     patch_rows = kv_cache.shape[2] // patch_total
     spots = jnp.concatenate([text_count, fresh_places, (offset // patch_rows)[None]])
     spots = spots.astype(jnp.int32)
-    line_0, spots = lax.optimization_barrier((line_0, spots))
-    left = along(line_0, 1, 1)
-    right = along(line_0, 1, -1)
-    cache, text, qkv_weight, qk_gain = after((kv_cache[0], text_kv[0], qkv_weight, qk_gain), line_0)
+    line_1 = first_round(normed_rows(after(entering, offset), 1, mod_rows))
+    low, high = joined_rows(line)
+    low, high, spots = lax.optimization_barrier((low, high, spots))
+    left_low = along(low, 1, 1)
+    right_high = along(high, 1, -1)
+    left_high = along(high, 1, 1)
+    right_low = along(low, 1, -1)
+    cache, text, qkv_weight, qk_gain = after((kv_cache[0], text_kv[0], qkv_weight, qk_gain), low)
     weight = qkv_weight[0].T
     packed_weight = packed_rows(weight, swapped(weight))
     gains = jnp.pad(qk_gain[0], ((0, 0), (0, HD)), constant_values=1.0)
     prepared = prepared_keys(spots, cache, text)
-    left, right, prepared, packed_weight, gains = lax.optimization_barrier(
-        (left, right, prepared, packed_weight, gains)
+    left_low, right_high, prepared, packed_weight, gains = lax.optimization_barrier(
+        (left_low, right_high, prepared, packed_weight, gains)
     )
 
     def project(pieces):
         own, other = projected_rows(pieces, packed_weight, gains)
         return own, swapped(other)
 
-    half = line_0.shape[0] // 2
-    far_low = along(left[:half], 1, 1)
-    far_high = along(right[half:], 1, -1)
-    own_near, other_near = project([line_0, left, right])
-    far_low, far_high, line_1 = lax.optimization_barrier((far_low, far_high, line_1))
+    far_low = along(left_low, 1, 1)
+    far_high = along(right_high, 1, -1)
+    own_near, other_near = project([low, high, left_low, left_high, right_low, right_high])
+    line_1 = after(jnp.concatenate(line_1, axis=0), far_low, far_high)
     left_1 = along(line_1, 1, 1)
     right_1 = along(line_1, 1, -1)
     far_1 = along(line_1, 1, 2)

time: 341 us -> 335 us (0.982)
  waiting for transfers between devices: 32.1 us -> 18.2 us
  Pallas kernels: 249 us -> 256 us
  local copies, waits for them, and re-layouts: 9.85 us -> 3.04 us
  starting transfers between devices: 26.5 us -> 32.2 us
    ppermute x10 -> x15, waiting for transfers between devices: 15.1 us -> 1.13 us  [along(): return lax.ppermute(value, 'seq', pairs_of(phase, step))]
    ppermute x10 -> x15, starting transfers between devices: 15.1 us -> 23.9 us  [along(): return lax.ppermute(value, 'seq', pairs_of(phase, step))]
    unnamed x34 -> x24, local copies, waits for them, and re-layouts: 9.43 us -> 2.7 us
    pallas_call x1, Pallas kernels: 3.27 us -> 7.12 us  [prepared_keys(): pl.pallas_call(prepare_kernel, out_shape=(jax.ShapeDtypeStruct((branches,...]
  transfers between devices with their start and end apart: 15 -> 20, of which waited for: 7 -> 5; matrix products, arithmetic and copies ran while one was open for 0% -> 1% of each run, Pallas kernels for 37% -> 40%
where the time goes in v2:
time: 335 us
  Pallas kernels  256 us (76%)
  starting transfers between devices  32.2 us (10%)
  waiting for transfers between devices  18.2 us (5%)
  blocking collectives  17.4 us (5%)
  between operations  4.23 us (1%)
  other arithmetic  3.49 us (1%)
    pallas_call x2, Pallas kernels, attended_rows(): pl.pallas_call(functools.partial(attend_kernel, (len(own_pieces), len(oth...  233 us
    ppermute x15, starting transfers between devices, along(): return lax.ppermute(value, 'seq', pairs_of(phase, step))  23.9 us
    all_to_all x1, blocking collectives, local(): lax.all_to_all(attended, 'seq', split_axis=0, concat_axis=0, tiled=True)  17.4 us
    ppermute x1, waiting for transfers between devices, local(): lax.ppermute(done, 'section', [(i, (i + 1) % count) for i in range(count)])  15.2 us
    pallas_call x3, Pallas kernels, projected_rows(): pl.pallas_call(project_kernel, out_shape=(out, out), compiler_params=pltp...  11.8 us
    pallas_call x1, Pallas kernels, prepared_keys(): pl.pallas_call(prepare_kernel, out_shape=(jax.ShapeDtypeStruct((branches,...  7.12 us
    ppermute x4, starting transfers between devices, swapped(): return lax.ppermute(value, 'seq', [(i, i ^ 1) for i in range(2 * CHIPS)])  6.89 us
  transfers between devices with their start and end apart: 20, of which 5 were waited for; matrix products, arithmetic and copies ran while one was open for 1% of the time, Pallas kernels for 40%

profile of v2, /device:TPU:1, one launch (start us, length us, event | category | flops | bytes accessed | tf_op | source)
XLA Modules:
  0.0 334.8 jit_solution(152095835415100395)
XLA Ops:
  1.4 1.1 copy-done
  2.8 4.5 %collective-permute-start.2 = (bf16[64,2432]{1,0:T(8,128)(2,1)S(1)}, bf16[64,2432]{1,0:T(8,128)(2,1)S(1)}, u32[]{:S(2)}, u32[]{:S(2)}) collective-permute-start(bf16[64,2432]{1,0:T(8,128)(2,1)S(1)} %shard_map.122.refs_0_), channel_id=1, source_target_pairs={{0,4},{1,17},{2,6},{3,19},{4,0},{5,21},{6,2},{7,23},{8,12},{9,25},... | collective-permute-start | bytes 933896 | tf_op jit(solution)/shard_map/ppermute | solution.py:32
  7.7 1.0 collective-permute-start
  9.4 1.3 fusion.4
  14.6 1.3 pad_add_fusion.spots
  17.6 1.9 collective-permute-start.7
  19.8 2.4 collective-permute-start.15
  22.3 7.1 %shard_map.125 = (bf16[2,6400,256]{2,1,0:T(8,128)(2,1)}, bf16[2,6400,128]{2,1,0:T(8,128)(2,1)}, f32[2,1,128]{2,1,0:T(1,128)}) custom-call(s32[35]{0:T(128)} %pad_add_fusion.spots, bf16[2,8192,128]{2,1,0:T(8,128)(2,1)} %bitcast.27, bf16[2,8192,128]{2,1,0:T(8,128)(2,1)} %bitcast.28, bf16[2,8192,128]{2,1,0:T(8,128)(2,1)} %bitcast.29, bf16[2,256,128]{2,1,0:T(8,128)(2,1)} %bitcast.31), custom_call_target="tpu_custom_call" | custom-call | flops 419430400 | bytes 13107200 | tf_op jit(solution)/shard_map/pallas_call | solution.py:192
  30.2 2.7 collective-permute-start.10
  33.2 3.4 %collective-permute-start.5 = (bf16[64,2432]{1,0:T(8,128)(2,1)S(1)}, bf16[64,2432]{1,0:T(8,128)(2,1)S(1)}, u32[]{:S(2)}, u32[]{:S(2)}) collective-permute-start(bf16[64,2432]{1,0:T(8,128)(2,1)S(1)} %shard_map.124), channel_id=1, source_target_pairs={{0,4},{1,17},{2,6},{3,19},{4,0},{5,21},{6,2},{7,23},{8,12},{9,25},... | collective-permute-start | bytes 933896 | tf_op jit(solution)/shard_map/ppermute | solution.py:32
  36.9 3.5 %collective-permute-start.4 = (bf16[64,2432]{1,0:T(8,128)(2,1)S(1)}, bf16[64,2432]{1,0:T(8,128)(2,1)S(1)}, u32[]{:S(2)}, u32[]{:S(2)}) collective-permute-start(bf16[64,2432]{1,0:T(8,128)(2,1)S(1)} %shard_map.124), channel_id=1, source_target_pairs={{0,6},{1,25},{2,0},{3,27},{4,2},{5,29},{6,4},{7,31},{8,14},{9,1},{... | collective-permute-start | bytes 933896 | tf_op jit(solution)/shard_map/ppermute | solution.py:32
  40.4 6.8 %shard_map.127 = (bf16[768,256]{1,0:T(8,128)(2,1)S(1)}, bf16[768,256]{1,0:T(8,128)(2,1)S(1)}) custom-call(bf16[128,2432]{1,0:T(8,128)(2,1)S(1)} %get-tuple-element.48.refs_0_, bf16[128,2432]{1,0:T(8,128)(2,1)} %get-tuple-element.49.refs_1_, bf16[128,2432]{1,0:T(8,128)(2,1)} %collective-permute-done.6.refs_2_, ...), custom_call_target="tpu_custom_call" | custom-call | flops 1912602624 | bytes 3735552 | tf_op jit(solution)/shard_map/pallas_call | solution.py:135
  47.2 5.8 %collective-permute-start.16 = (bf16[768,256]{1,0:T(8,128)(2,1)S(1)}, bf16[768,256]{1,0:T(8,128)(2,1)S(1)}, u32[]{:S(2)}, u32[]{:S(2)}) collective-permute-start(bf16[768,256]{1,0:T(8,128)(2,1)S(1)} %get-tuple-element.64), channel_id=1, source_target_pairs={{0,1},{1,0},{2,3},{3,2},{4,5},{5,4},{6,7},{7,6},{8,9},{9,8},{10,11... | collective-permute-start | bytes 1179656 | tf_op jit(solution)/shard_map/ppermute | solution.py:36
  53.1 1.8 shard_map.128
  55.2 2.3 collective-permute-start.13
  57.4 0.9 collective-permute-start.12
  58.9 116.1 %shard_map.129 = (bf16[32,64,128]{2,1,0:T(8,128)(2,1)S(1)}, bf16[2,2048,128]{2,1,0:T(8,128)(2,1)}) custom-call(s32[35]{0:T(128)S(1)} %copy-done.3, bf16[768,256]{1,0:T(8,128)(2,1)S(1)} %get-tuple-element.62.refs_0_, bf16[256,256]{1,0:T(8,128)(2,1)S(1)} %get-tuple-element.63.refs_1_, bf16[768,256]{1,0:T(8,128)(2,1)S(1)} %collective-permute-done.16.refs_2_, ...), custom_call_target="tpu_custom_call" | custom-call | flops 17716740096 | bytes 8388608 | tf_op jit(solution)/shard_map/pallas_call | solution.py:381
  175.1 3.1 shard_map.130
  178.5 1.9 collective-permute-done.18.refs_1_
  180.4 116.6 %shard_map.131 = (bf16[32,64,128]{2,1,0:T(8,128)(2,1)S(1)}, bf16[2,2048,128]{2,1,0:T(8,128)(2,1)}) custom-call(s32[35]{0:T(128)S(1)} %copy-done.3, bf16[1024,256]{1,0:T(8,128)(2,1)S(1)} %get-tuple-element.74.refs_0_, bf16[1024,256]{1,0:T(8,128)(2,1)S(1)} %collective-permute-done.18.refs_1_, ...), custom_call_target="tpu_custom_call", output_to_operand_aliasing={{0}: (6, {}), {1}: (7, {})} | custom-call | flops 17716740096 | bytes 8388608 | tf_op jit(solution)/shard_map/pallas_call | solution.py:381
  296.9 17.4 %all_to_all.5.heads = bf16[32,64,128]{2,1,0:T(8,128)(2,1)S(1)} all-to-all(bf16[32,64,128]{2,1,0:T(8,128)(2,1)S(1)} %get-tuple-element.78), channel_id=1, replica_groups=mesh['section'=4,'seq'=32] {'seq'}, dimensions={0} | all-to-all | bytes 1048576 | tf_op jit(solution)/shard_map/all_to_all | solution.py:559
  314.4 3.0 shard_map.132
  317.4 1.4 collective-permute-start.19
  318.8 15.2 %collective-permute-done.19 = bf16[2,64,2432]{2,1,0:T(8,128)(2,1)S(1)} collective-permute-done((bf16[2,64,2432]{2,1,0:T(8,128)(2,1)S(1)}, bf16[2,64,2432]{2,1,0:T(8,128)(2,1)S(1)}, u32[]{:S(2)}, u32[]{:S(2)}) %collective-permute-start.19) | collective-permute-done | bytes 622624 | tf_op jit(solution)/shard_map/ppermute | solution.py:562
  (63 shorter events, 8.0 us)
Async XLA Ops:
  0.6 21.6 %copy-start.7 = (f32[1,2,64]{2,1,0:T(2,128)S(1)}, f32[1,2,64]{2,1,0:T(2,128)}, u32[]{:S(2)}) copy-start(f32[1,2,64]{2,1,0:T(2,128)} %param.14) | copy-start | bytes 1540
  2.8 13.0 %collective-permute-start.2 = (bf16[64,2432]{1,0:T(8,128)(2,1)S(1)}, bf16[64,2432]{1,0:T(8,128)(2,1)S(1)}, u32[]{:S(2)}, u32[]{:S(2)}) collective-permute-start(bf16[64,2432]{1,0:T(8,128)(2,1)S(1)} %shard_map.122.refs_0_), channel_id=1, source_target_pairs={{0,4},{1,17},{2,6},{3,19},{4,0},{5,21},{6,2},{7,23},{8,12},{9,25},... | collective-permute-start | bytes 933896 | tf_op jit(solution)/shard_map/ppermute | solution.py:32
  7.3 8.7 %collective-permute-start.1 = (bf16[64,2432]{1,0:T(8,128)(2,1)S(1)}, bf16[64,2432]{1,0:T(8,128)(2,1)S(1)}, u32[]{:S(2)}, u32[]{:S(2)}) collective-permute-start(bf16[64,2432]{1,0:T(8,128)(2,1)S(1)} %shard_map.122.refs_0_), channel_id=1, source_target_pairs={{0,6},{1,25},{2,0},{3,27},{4,2},{5,29},{6,4},{7,31},{8,14},{9,1},{... | collective-permute-start | bytes 933896 | tf_op jit(solution)/shard_map/ppermute | solution.py:32
  7.7 8.3 %collective-permute-start = (bf16[64,2432]{1,0:T(8,128)(2,1)S(1)}, bf16[64,2432]{1,0:T(8,128)(2,1)S(1)}, u32[]{:S(2)}, u32[]{:S(2)}) collective-permute-start(bf16[64,2432]{1,0:T(8,128)(2,1)S(1)} %shard_map.122.refs_0_), channel_id=1, source_target_pairs={{0,2},{1,9},{2,4},{3,11},{4,6},{5,13},{6,0},{7,15},{8,10},{9,17},{... | collective-permute-start | bytes 933896 | tf_op jit(solution)/shard_map/ppermute | solution.py:32
  16.9 12.4 %collective-permute-start.8 = (bf16[192,2432]{1,0:T(8,128)(2,1)}, bf16[192,2432]{1,0:T(8,128)(2,1)S(1)}, u32[]{:S(2)}, u32[]{:S(2)}) collective-permute-start(bf16[192,2432]{1,0:T(8,128)(2,1)} %bitcast.22), channel_id=1, source_target_pairs={{0,1},{1,0},{2,3},{3,2},{4,5},{5,4},{6,7},{7,6},{8,9},{9,8},{10,11... | collective-permute-start | bytes 2801672 | tf_op jit(solution)/shard_map/ppermute | solution.py:36
  17.6 12.0 %collective-permute-start.7 = (bf16[128,2432]{1,0:T(8,128)(2,1)}, bf16[128,2432]{1,0:T(8,128)(2,1)}, u32[]{:S(2)}, u32[]{:S(2)}) collective-permute-start(bf16[128,2432]{1,0:T(8,128)(2,1)} %get-tuple-element.49.refs_1_), channel_id=1, source_target_pairs={{0,24},{1,7},{2,26},{3,1},{4,28},{5,3},{6,30},{7,5},{8,0},{9,15},{... | collective-permute-start | bytes 1867784 | tf_op jit(solution)/shard_map/ppermute | solution.py:32
  19.5 10.7 %collective-permute-start.6 = (bf16[128,2432]{1,0:T(8,128)(2,1)S(1)}, bf16[128,2432]{1,0:T(8,128)(2,1)}, u32[]{:S(2)}, u32[]{:S(2)}) collective-permute-start(bf16[128,2432]{1,0:T(8,128)(2,1)S(1)} %get-tuple-element.48.refs_0_), channel_id=1, source_target_pairs={{0,8},{1,3},{2,10},{3,5},{4,12},{5,7},{6,14},{7,1},{8,16},{9,11},{... | collective-permute-start | bytes 1867784 | tf_op jit(solution)/shard_map/ppermute | solution.py:32
  19.5 17.4 %collective-permute-start.14 = (bf16[128,2432]{1,0:T(8,128)(2,1)}, bf16[128,2432]{1,0:T(8,128)(2,1)}, u32[]{:S(2)}, u32[]{:S(2)}) collective-permute-start(bf16[128,2432]{1,0:T(8,128)(2,1)} %get-tuple-element.49.refs_1_), channel_id=1, source_target_pairs={{0,8},{1,3},{2,10},{3,5},{4,12},{5,7},{6,14},{7,1},{8,16},{9,11},{... | collective-permute-start | bytes 1867784 | tf_op jit(solution)/shard_map/ppermute | solution.py:32
  19.8 20.6 %collective-permute-start.15 = (bf16[128,2432]{1,0:T(8,128)(2,1)S(1)}, bf16[128,2432]{1,0:T(8,128)(2,1)}, u32[]{:S(2)}, u32[]{:S(2)}) collective-permute-start(bf16[128,2432]{1,0:T(8,128)(2,1)S(1)} %get-tuple-element.48.refs_0_), channel_id=1, source_target_pairs={{0,24},{1,7},{2,26},{3,1},{4,28},{5,3},{6,30},{7,5},{8,0},{9,15},{... | collective-permute-start | bytes 1867784 | tf_op jit(solution)/shard_map/ppermute | solution.py:32
  30.2 17.0 %collective-permute-start.9 = (bf16[128,2432]{1,0:T(8,128)(2,1)}, bf16[128,2432]{1,0:T(8,128)(2,1)S(1)}, u32[]{:S(2)}, u32[]{:S(2)}) collective-permute-start(bf16[128,2432]{1,0:T(8,128)(2,1)} %collective-permute-done.6.refs_2_), channel_id=1, source_target_pairs={{0,8},{1,3},{2,10},{3,5},{4,12},{5,7},{6,14},{7,1},{8,16},{9,11},{... | collective-permute-start | bytes 1867784 | tf_op jit(solution)/shard_map/ppermute | solution.py:32
  30.2 22.9 %collective-permute-start.10 = (bf16[128,2432]{1,0:T(8,128)(2,1)}, bf16[128,2432]{1,0:T(8,128)(2,1)S(1)}, u32[]{:S(2)}, u32[]{:S(2)}) collective-permute-start(bf16[128,2432]{1,0:T(8,128)(2,1)} %collective-permute-done.7.refs_5_), channel_id=1, source_target_pairs={{0,24},{1,7},{2,26},{3,1},{4,28},{5,3},{6,30},{7,5},{8,0},{9,15},{... | collective-permute-start | bytes 1867784 | tf_op jit(solution)/shard_map/ppermute | solution.py:32
  33.2 21.8 %collective-permute-start.5 = (bf16[64,2432]{1,0:T(8,128)(2,1)S(1)}, bf16[64,2432]{1,0:T(8,128)(2,1)S(1)}, u32[]{:S(2)}, u32[]{:S(2)}) collective-permute-start(bf16[64,2432]{1,0:T(8,128)(2,1)S(1)} %shard_map.124), channel_id=1, source_target_pairs={{0,4},{1,17},{2,6},{3,19},{4,0},{5,21},{6,2},{7,23},{8,12},{9,25},... | collective-permute-start | bytes 933896 | tf_op jit(solution)/shard_map/ppermute | solution.py:32
  36.9 18.1 %collective-permute-start.4 = (bf16[64,2432]{1,0:T(8,128)(2,1)S(1)}, bf16[64,2432]{1,0:T(8,128)(2,1)S(1)}, u32[]{:S(2)}, u32[]{:S(2)}) collective-permute-start(bf16[64,2432]{1,0:T(8,128)(2,1)S(1)} %shard_map.124), channel_id=1, source_target_pairs={{0,6},{1,25},{2,0},{3,27},{4,2},{5,29},{6,4},{7,31},{8,14},{9,1},{... | collective-permute-start | bytes 933896 | tf_op jit(solution)/shard_map/ppermute | solution.py:32
  40.4 14.7 %collective-permute-start.3 = (bf16[64,2432]{1,0:T(8,128)(2,1)S(1)}, bf16[64,2432]{1,0:T(8,128)(2,1)S(1)}, u32[]{:S(2)}, u32[]{:S(2)}) collective-permute-start(bf16[64,2432]{1,0:T(8,128)(2,1)S(1)} %shard_map.124), channel_id=1, source_target_pairs={{0,2},{1,9},{2,4},{3,11},{4,6},{5,13},{6,0},{7,15},{8,10},{9,17},{... | collective-permute-start | bytes 933896 | tf_op jit(solution)/shard_map/ppermute | solution.py:32
  47.2 11.7 %collective-permute-start.16 = (bf16[768,256]{1,0:T(8,128)(2,1)S(1)}, bf16[768,256]{1,0:T(8,128)(2,1)S(1)}, u32[]{:S(2)}, u32[]{:S(2)}) collective-permute-start(bf16[768,256]{1,0:T(8,128)(2,1)S(1)} %get-tuple-element.64), channel_id=1, source_target_pairs={{0,1},{1,0},{2,3},{3,2},{4,5},{5,4},{6,7},{7,6},{8,9},{9,8},{10,11... | collective-permute-start | bytes 1179656 | tf_op jit(solution)/shard_map/ppermute | solution.py:36
  54.9 4.0 %collective-permute-start.17 = (bf16[256,256]{1,0:T(8,128)(2,1)S(1)}, bf16[256,256]{1,0:T(8,128)(2,1)S(1)}, u32[]{:S(2)}, u32[]{:S(2)}) collective-permute-start(bf16[256,256]{1,0:T(8,128)(2,1)S(1)} %get-tuple-element.65), channel_id=1, source_target_pairs={{0,1},{1,0},{2,3},{3,2},{4,5},{5,4},{6,7},{7,6},{8,9},{9,8},{10,11... | collective-permute-start | bytes 393224 | tf_op jit(solution)/shard_map/ppermute | solution.py:36
  55.2 119.9 %collective-permute-start.13 = (bf16[256,2432]{1,0:T(8,128)(2,1)S(1)}, bf16[256,2432]{1,0:T(8,128)(2,1)S(1)}, u32[]{:S(2)}, u32[]{:S(2)}) collective-permute-start(bf16[256,2432]{1,0:T(8,128)(2,1)S(1)} %pad_maximum_fusion.refs_0_), channel_id=1, source_target_pairs={{0,16},{1,5},{2,18},{3,7},{4,20},{5,1},{6,22},{7,3},{8,24},{9,13},... | collective-permute-start | bytes 3735560 | tf_op jit(solution)/shard_map/ppermute | solution.py:32
  57.4 117.6 %collective-permute-start.12 = (bf16[256,2432]{1,0:T(8,128)(2,1)S(1)}, bf16[256,2432]{1,0:T(8,128)(2,1)S(1)}, u32[]{:S(2)}, u32[]{:S(2)}) collective-permute-start(bf16[256,2432]{1,0:T(8,128)(2,1)S(1)} %pad_maximum_fusion.refs_0_), channel_id=1, source_target_pairs={{0,24},{1,7},{2,26},{3,1},{4,28},{5,3},{6,30},{7,5},{8,0},{9,15},{... | collective-permute-start | bytes 3735560 | tf_op jit(solution)/shard_map/ppermute | solution.py:32
  58.4 116.7 %collective-permute-start.11 = (bf16[256,2432]{1,0:T(8,128)(2,1)S(1)}, bf16[256,2432]{1,0:T(8,128)(2,1)S(1)}, u32[]{:S(2)}, u32[]{:S(2)}) collective-permute-start(bf16[256,2432]{1,0:T(8,128)(2,1)S(1)} %pad_maximum_fusion.refs_0_), channel_id=1, source_target_pairs={{0,8},{1,3},{2,10},{3,5},{4,12},{5,7},{6,14},{7,1},{8,16},{9,11},{... | collective-permute-start | bytes 3735560 | tf_op jit(solution)/shard_map/ppermute | solution.py:32
  178.2 2.2 collective-permute-start.18
  180.4 134.0 %slice-start = ((s8[9961472]{0:T(1024)(128)(4,1)}), s8[4194304]{0:T(1024)(128)(4,1)S(1)}, s32[]{:S(2)}) async-start(s8[9961472]{0:T(1024)(128)(4,1)} %bitcast.16), calls=%async_computation.1 | async-start | bytes 8388608
  180.4 134.0 %slice-start.1 = ((s8[9961472]{0:T(1024)(128)(4,1)}), s8[4194304]{0:T(1024)(128)(4,1)S(1)}, s32[]{:S(2)}) async-start(s8[9961472]{0:T(1024)(128)(4,1)} %bitcast.16), calls=%async_computation.2 | async-start | bytes 8388608
  180.4 134.0 %slice-start.2 = ((s8[9961472]{0:T(1024)(128)(4,1)}), s8[1572864]{0:T(1024)(128)(4,1)S(1)}, s32[]{:S(2)}) async-start(s8[9961472]{0:T(1024)(128)(4,1)} %bitcast.16), calls=%async_computation.3 | async-start | bytes 3145728
  317.4 16.6 %collective-permute-start.19 = (bf16[2,64,2432]{2,1,0:T(8,128)(2,1)S(1)}, bf16[2,64,2432]{2,1,0:T(8,128)(2,1)S(1)}, u32[]{:S(2)}, u32[]{:S(2)}) collective-permute-start(bf16[2,64,2432]{2,1,0:T(8,128)(2,1)S(1)} %shard_map.132), channel_id=1, source_target_pairs={{0,32},{32,64},{64,96},{96,0},{1,33},{33,65},{65,97},{97,1},{2,34}... | collective-permute-start | bytes 1867784 | tf_op jit(solution)/shard_map/ppermute | solution.py:562
  (7 other events, 52.2 us)

commit v3 on v2

--- a/solution.py
+++ b/solution.py
@@ -97,18 +97,17 @@
     )(*parts)
 
 
-def project_kernel(*refs):
-    pieces = refs[:-4]
-    weight, gains, own_ref, other_ref = refs[-4:]
+def project_kernel(count, *refs):
+    pieces = refs[:count]
+    weight, gains, own_ref, other_ref, joined = refs[count:]
     lane = lax.broadcasted_iota(jnp.int32, (1, 2 * HD), 1)
     query_gain = gains[0:1, :]
     key_gain = gains[1:2, :]
-    row = 0
-    for piece in pieces:
-        rows = piece.shape[0]
+
+    def block(rows, here):
         for part, out_ref in ((0, own_ref), (4 * HD, other_ref)):
             out = lax.dot_general(
-                piece[...],
+                rows,
                 weight[part : part + 4 * HD, :],
                 (((1,), (1,)), ((), ())),
                 preferred_element_type=jnp.float32,
@@ -118,23 +117,39 @@
             key_square = jnp.where(lane < HD, kv * kv, 0.0)
             key_mean = jnp.sum(key_square, axis=-1, keepdims=True) * (1.0 / HD)
             key_scaled = kv * lax.rsqrt(key_mean + 1e-06) * key_gain
-            out_ref[row : row + rows, : 2 * HD] = jnp.where(lane < HD, key_scaled, kv).astype(
+            out_ref[here, : 2 * HD] = jnp.where(lane < HD, key_scaled, kv).astype(jnp.bfloat16)
+            query_mean = jnp.sum(q * q, axis=-1, keepdims=True) * (1.0 / HD)
+            out_ref[here, 2 * HD :] = (q * lax.rsqrt(query_mean + 1e-06) * query_gain).astype(
                 jnp.bfloat16
             )
-            query_mean = jnp.sum(q * q, axis=-1, keepdims=True) * (1.0 / HD)
-            out_ref[row : row + rows, 2 * HD :] = (
-                q * lax.rsqrt(query_mean + 1e-06) * query_gain
-            ).astype(jnp.bfloat16)
-        row += rows
+
+    row = 0
+    if pieces[0].shape[0] == joined.shape[0]:
+        for piece in pieces:
+            block(piece[...], slice(row, row + piece.shape[0]))
+            row += piece.shape[0]
+        return
+
+    step = 4 * HD
+    for piece in pieces:
+        joined[row : row + piece.shape[0], :] = piece[...]
+        row += piece.shape[0]
+
+    @pl.loop(0, row // step)
+    def _(i):
+        here = pl.ds(pl.multiple_of(i * step, step), step)
+        block(joined[here, :], here)
 
 
 def projected_rows(pieces, packed_weight, gains):
     rows = sum(piece.shape[0] for piece in pieces)
     width = packed_weight.shape[1]
     out = jax.ShapeDtypeStruct((rows, 4 * HD), jnp.bfloat16)
-    return pl.pallas_call(
-        project_kernel,
+    large = pieces[0].shape[0] == 4 * HD
+    return pl.pallas_call(
+        functools.partial(project_kernel, len(pieces)),
         out_shape=(out, out),
+        scratch_shapes=[pltpu.VMEM((4 * HD if large else rows, width), jnp.bfloat16)],
         compiler_params=pltpu.CompilerParams(vmem_limit_bytes=40 * MIB),
         cost_estimate=pl.CostEstimate(
             flops=2 * rows * width * 512, bytes_accessed=rows * width * 2, transcendentals=0
@@ -407,64 +422,35 @@
     )(spots, *pieces, *prepared, *earlier)
 
 
-def finish_kernel(heads, weight, entering, gate, out_ref, lhs, total):
-    step = pl.program_id(0)
+def finish_kernel(columns, heads, weight, entering, gate, out_ref, lhs):
     rows = entering.shape[1]
     lane = lax.broadcasted_iota(jnp.int32, (1, 2 * HD), 1)
-
-    @pl.when(step == 0)
-    def _():
-        for pair in range(CHIPS):
-            low = heads[2 * pair].astype(jnp.float32)
-            high = heads[2 * pair + 1].astype(jnp.float32)
-            top = jnp.where(lane < HD, low, pltpu.roll(high, HD, 1)).astype(jnp.bfloat16)
-            bottom = jnp.where(lane < HD, pltpu.roll(low, HD, 1), high).astype(jnp.bfloat16)
-            at = (pair % SIDE) * 2 * HD
-            for branch in range(2):
-                from_row = branch * rows // 2
-                to = branch * rows
-                here = slice(at, at + 2 * HD)
-                part = slice(from_row, from_row + rows // 2)
-                lhs[pair // SIDE, to : to + rows // 2, here] = top[part]
-                lhs[pair // SIDE, to + rows // 2 : to + rows, here] = bottom[part]
-
-    part = jnp.dot(lhs[step], weight[...], preferred_element_type=jnp.float32)
-
-    @pl.when(step == 0)
-    def _():
-        total[...] = part
-
-    @pl.when(step > 0)
-    def _():
-        total[...] += part
-
-    @pl.when(step == SIDE - 1)
-    def _():
+    for pair in range(CHIPS):
+        low = heads[2 * pair].astype(jnp.float32)
+        high = heads[2 * pair + 1].astype(jnp.float32)
+        top = jnp.where(lane < HD, low, pltpu.roll(high, HD, 1)).astype(jnp.bfloat16)
+        bottom = jnp.where(lane < HD, pltpu.roll(low, HD, 1), high).astype(jnp.bfloat16)
+        here = slice(pair * 2 * HD, (pair + 1) * 2 * HD)
         for branch in range(2):
-            sums = total[branch * rows : (branch + 1) * rows, :]
-            out_ref[branch] = (entering[branch].astype(jnp.float32) + gate[2:3, :] * sums).astype(
-                jnp.bfloat16
-            )
-
-
-def finished_rows(heads, weight, entering, mod_rows):
-    rows, width = entering.shape[1:]
-    depth = weight.shape[0] // SIDE
-    return pl.pallas_call(
-        finish_kernel,
-        out_shape=jax.ShapeDtypeStruct(entering.shape, jnp.bfloat16),
-        grid=(SIDE,),
-        in_specs=[
-            pl.BlockSpec(heads.shape, lambda i: (0, 0, 0)),
-            pl.BlockSpec((depth, width), lambda i: (i, 0)),
-            pl.BlockSpec(entering.shape, lambda i: (0, 0, 0)),
-            pl.BlockSpec((3, width), lambda i: (0, 0)),
-        ],
-        out_specs=pl.BlockSpec(entering.shape, lambda i: (0, 0, 0)),
-        scratch_shapes=[
-            pltpu.VMEM((SIDE, 2 * rows, depth), jnp.bfloat16),
-            pltpu.VMEM((2 * rows, width), jnp.float32),
-        ],
+            to = branch * rows
+            part = slice(branch * rows // 2, (branch + 1) * rows // 2)
+            lhs[to : to + rows // 2, here] = top[part]
+            lhs[to + rows // 2 : to + rows, here] = bottom[part]
+    sums = jnp.dot(lhs[...], weight[:, columns], preferred_element_type=jnp.float32)
+    for branch in range(2):
+        part = sums[branch * rows : (branch + 1) * rows]
+        out_ref[branch] = (
+            entering[branch, :, columns].astype(jnp.float32) + gate[2:3, columns] * part
+        ).astype(jnp.bfloat16)
+
+
+def finished_rows(heads, weight, entering, mod_rows, columns):
+    branches, rows = entering.shape[:2]
+    width = columns.stop - columns.start
+    return pl.pallas_call(
+        functools.partial(finish_kernel, columns),
+        out_shape=jax.ShapeDtypeStruct((branches, rows, width), jnp.bfloat16),
+        scratch_shapes=[pltpu.VMEM((branches * rows, weight.shape[0]), jnp.bfloat16)],
         compiler_params=pltpu.CompilerParams(vmem_limit_bytes=24 * MIB),
         cost_estimate=pl.CostEstimate(
             flops=4 * rows * width * weight.shape[0],
@@ -557,9 +543,14 @@
     attended, fresh = attended_rows(spots, 1, (own_all,), (other_all,), prepared, first)
 
     heads = lax.all_to_all(attended, "seq", split_axis=0, concat_axis=0, tiled=True)
-    done = finished_rows(heads, out_weight[0], entering, mod_rows)
     count = lax.axis_size("section")
-    moved = lax.ppermute(done, "section", [(i, (i + 1) % count) for i in range(count)])
+    width = entering.shape[2]
+    cut = width // 256 * 128 + 128
+    moved = []
+    for columns in (slice(0, cut), slice(cut, width)):
+        done = finished_rows(heads, out_weight[0], entering, mod_rows, columns)
+        moved.append(lax.ppermute(done, "section", [(i, (i + 1) % count) for i in range(count)]))
+    moved = jnp.concatenate(moved, axis=-1)
     return (moved[None], fresh[None])
 
 

time: 335 us -> 332 us (level)
    pallas_call x4 -> x5, Pallas kernels: 14.7 us -> 11.3 us  [the longest x3 9.31 us: projected_rows(): pl.pallas_call(functools.partial(project_kernel, len(pieces)), out_shape=...]
    ppermute x1 -> x2, waiting for transfers between devices: 15.2 us -> 12.9 us  [local(): lax.ppermute(done, 'section', [(i, (i + 1) % count) for i in range(count)])]
  transfers between devices with their start and end apart: 20 -> 21, of which waited for: 5 -> 6; matrix products, arithmetic and copies ran while one was open for 1% -> 1% of each run, Pallas kernels for 40% -> 39%
where the time goes in v3:
time: 332 us
  Pallas kernels  253 us (76%)
  starting transfers between devices  34 us (10%)
  waiting for transfers between devices  17.2 us (5%)
  blocking collectives  17.1 us (5%)
  other arithmetic  4.32 us (1%)
  between operations  4.21 us (1%)
    pallas_call x2, Pallas kernels, attended_rows(): pl.pallas_call(functools.partial(attend_kernel, (len(own_pieces), len(oth...  233 us
    ppermute x15, starting transfers between devices, along(): return lax.ppermute(value, 'seq', pairs_of(phase, step))  23.9 us
    all_to_all x1, blocking collectives, local(): lax.all_to_all(attended, 'seq', split_axis=0, concat_axis=0, tiled=True)  17.1 us
    ppermute x2, waiting for transfers between devices, local(): lax.ppermute(done, 'section', [(i, (i + 1) % count) for i in range(count)])  12.9 us
    pallas_call x3, Pallas kernels, projected_rows(): pl.pallas_call(functools.partial(project_kernel, len(pieces)), out_shape=...  9.31 us
    ppermute x4, starting transfers between devices, swapped(): return lax.ppermute(value, 'seq', [(i, i ^ 1) for i in range(2 * CHIPS)])  7.34 us
    pallas_call x1, Pallas kernels, prepared_keys(): pl.pallas_call(prepare_kernel, out_shape=(jax.ShapeDtypeStruct((branches,...  7.11 us
  transfers between devices with their start and end apart: 21, of which 6 were waited for; matrix products, arithmetic and copies ran while one was open for 1% of the time, Pallas kernels for 39%

profile of v3, /device:TPU:1, one launch (start us, length us, event | category | flops | bytes accessed | tf_op | source)
XLA Modules:
  0.0 331.7 jit_solution(10788957792437920168)
XLA Ops:
  1.4 1.1 copy-done
  2.8 4.5 %collective-permute-start.2 = (bf16[64,2432]{1,0:T(8,128)(2,1)S(1)}, bf16[64,2432]{1,0:T(8,128)(2,1)S(1)}, u32[]{:S(2)}, u32[]{:S(2)}) collective-permute-start(bf16[64,2432]{1,0:T(8,128)(2,1)S(1)} %shard_map.122.refs_0_), channel_id=1, source_target_pairs={{0,4},{1,17},{2,6},{3,19},{4,0},{5,21},{6,2},{7,23},{8,12},{9,25},... | collective-permute-start | bytes 933896 | tf_op jit(solution)/shard_map/ppermute | solution.py:32
  7.7 1.0 collective-permute-start
  9.4 1.3 fusion.4
  14.6 1.2 pad_add_fusion.spots
  17.6 1.9 collective-permute-start.7
  19.8 2.4 collective-permute-start.15
  22.3 7.1 %shard_map.125 = (bf16[2,6400,256]{2,1,0:T(8,128)(2,1)}, bf16[2,6400,128]{2,1,0:T(8,128)(2,1)}, f32[2,1,128]{2,1,0:T(1,128)}) custom-call(s32[35]{0:T(128)} %pad_add_fusion.spots, bf16[2,8192,128]{2,1,0:T(8,128)(2,1)} %bitcast.31, bf16[2,8192,128]{2,1,0:T(8,128)(2,1)} %bitcast.32, bf16[2,8192,128]{2,1,0:T(8,128)(2,1)} %bitcast.33, bf16[2,256,128]{2,1,0:T(8,128)(2,1)} %bitcast.34), custom_call_target="tpu_custom_call" | custom-call | flops 419430400 | bytes 13107200 | tf_op jit(solution)/shard_map/pallas_call | solution.py:207
  30.2 2.7 collective-permute-start.10
  33.2 3.4 %collective-permute-start.5 = (bf16[64,2432]{1,0:T(8,128)(2,1)S(1)}, bf16[64,2432]{1,0:T(8,128)(2,1)S(1)}, u32[]{:S(2)}, u32[]{:S(2)}) collective-permute-start(bf16[64,2432]{1,0:T(8,128)(2,1)S(1)} %shard_map.124), channel_id=1, source_target_pairs={{0,4},{1,17},{2,6},{3,19},{4,0},{5,21},{6,2},{7,23},{8,12},{9,25},... | collective-permute-start | bytes 933896 | tf_op jit(solution)/shard_map/ppermute | solution.py:32
  36.9 3.5 %collective-permute-start.4 = (bf16[64,2432]{1,0:T(8,128)(2,1)S(1)}, bf16[64,2432]{1,0:T(8,128)(2,1)S(1)}, u32[]{:S(2)}, u32[]{:S(2)}) collective-permute-start(bf16[64,2432]{1,0:T(8,128)(2,1)S(1)} %shard_map.124), channel_id=1, source_target_pairs={{0,6},{1,25},{2,0},{3,27},{4,2},{5,29},{6,4},{7,31},{8,14},{9,1},{... | collective-permute-start | bytes 933896 | tf_op jit(solution)/shard_map/ppermute | solution.py:32
  40.4 5.2 %shard_map.127 = (bf16[768,256]{1,0:T(8,128)(2,1)S(1)}, bf16[768,256]{1,0:T(8,128)(2,1)S(1)}) custom-call(bf16[128,2432]{1,0:T(8,128)(2,1)S(1)} %get-tuple-element.48.refs_0_, bf16[128,2432]{1,0:T(8,128)(2,1)} %get-tuple-element.49.refs_1_, bf16[128,2432]{1,0:T(8,128)(2,1)} %collective-permute-done.6.refs_2_, ...), custom_call_target="tpu_custom_call" | custom-call | flops 1912602624 | bytes 3735552 | tf_op jit(solution)/shard_map/pallas_call | solution.py:149
  45.5 1.3 collective-permute-done.9.refs_0_
  46.8 6.3 %collective-permute-start.16 = (bf16[768,256]{1,0:T(8,128)(2,1)S(1)}, bf16[768,256]{1,0:T(8,128)(2,1)S(1)}, u32[]{:S(2)}, u32[]{:S(2)}) collective-permute-start(bf16[768,256]{1,0:T(8,128)(2,1)S(1)} %get-tuple-element.64), channel_id=1, source_target_pairs={{0,1},{1,0},{2,3},{3,2},{4,5},{5,4},{6,7},{7,6},{8,9},{9,8},{10,11... | collective-permute-start | bytes 1179656 | tf_op jit(solution)/shard_map/ppermute | solution.py:36
  53.1 1.0 shard_map.128
  54.4 2.3 collective-permute-start.13
  58.2 116.1 %shard_map.129 = (bf16[32,64,128]{2,1,0:T(8,128)(2,1)S(1)}, bf16[2,2048,128]{2,1,0:T(8,128)(2,1)}) custom-call(s32[35]{0:T(128)S(1)} %copy-done.3, bf16[768,256]{1,0:T(8,128)(2,1)S(1)} %get-tuple-element.62.refs_0_, bf16[256,256]{1,0:T(8,128)(2,1)S(1)} %get-tuple-element.63.refs_1_, bf16[768,256]{1,0:T(8,128)(2,1)S(1)} %collective-permute-done.16.refs_2_, ...), custom_call_target="tpu_custom_call" | custom-call | flops 17716740096 | bytes 8388608 | tf_op jit(solution)/shard_map/pallas_call | solution.py:396
  174.3 3.1 shard_map.130
  177.7 1.9 collective-permute-done.18.refs_1_
  179.6 116.6 %shard_map.131 = (bf16[32,64,128]{2,1,0:T(8,128)(2,1)S(1)}, bf16[2,2048,128]{2,1,0:T(8,128)(2,1)}) custom-call(s32[35]{0:T(128)S(1)} %copy-done.3, bf16[1024,256]{1,0:T(8,128)(2,1)S(1)} %get-tuple-element.74.refs_0_, bf16[1024,256]{1,0:T(8,128)(2,1)S(1)} %collective-permute-done.18.refs_1_, ...), custom_call_target="tpu_custom_call", output_to_operand_aliasing={{0}: (6, {}), {1}: (7, {})} | custom-call | flops 17716740096 | bytes 8388608 | tf_op jit(solution)/shard_map/pallas_call | solution.py:396
  296.2 17.1 %all_to_all.5.heads = bf16[32,64,128]{2,1,0:T(8,128)(2,1)S(1)} all-to-all(bf16[32,64,128]{2,1,0:T(8,128)(2,1)S(1)} %get-tuple-element.78), channel_id=1, replica_groups=mesh['section'=4,'seq'=32] {'seq'}, dimensions={0} | all-to-all | bytes 1048576 | tf_op jit(solution)/shard_map/all_to_all | solution.py:545
  314.3 1.4 collective-permute-start.19
  316.6 1.4 collective-permute-start.20
  318.0 12.8 %collective-permute-done.20 = bf16[2,64,1152]{2,1,0:T(8,128)(2,1)S(1)} collective-permute-done((bf16[2,64,1152]{2,1,0:T(8,128)(2,1)S(1)}, bf16[2,64,1152]{2,1,0:T(8,128)(2,1)S(1)}, u32[]{:S(2)}, u32[]{:S(2)}) %collective-permute-start.20) | collective-permute-done | bytes 294944 | tf_op jit(solution)/shard_map/ppermute | solution.py:552
  (66 shorter events, 11.0 us)
Async XLA Ops:
  2.8 13.0 %collective-permute-start.2 = (bf16[64,2432]{1,0:T(8,128)(2,1)S(1)}, bf16[64,2432]{1,0:T(8,128)(2,1)S(1)}, u32[]{:S(2)}, u32[]{:S(2)}) collective-permute-start(bf16[64,2432]{1,0:T(8,128)(2,1)S(1)} %shard_map.122.refs_0_), channel_id=1, source_target_pairs={{0,4},{1,17},{2,6},{3,19},{4,0},{5,21},{6,2},{7,23},{8,12},{9,25},... | collective-permute-start | bytes 933896 | tf_op jit(solution)/shard_map/ppermute | solution.py:32
  7.3 8.7 %collective-permute-start.1 = (bf16[64,2432]{1,0:T(8,128)(2,1)S(1)}, bf16[64,2432]{1,0:T(8,128)(2,1)S(1)}, u32[]{:S(2)}, u32[]{:S(2)}) collective-permute-start(bf16[64,2432]{1,0:T(8,128)(2,1)S(1)} %shard_map.122.refs_0_), channel_id=1, source_target_pairs={{0,6},{1,25},{2,0},{3,27},{4,2},{5,29},{6,4},{7,31},{8,14},{9,1},{... | collective-permute-start | bytes 933896 | tf_op jit(solution)/shard_map/ppermute | solution.py:32
  7.7 8.3 %collective-permute-start = (bf16[64,2432]{1,0:T(8,128)(2,1)S(1)}, bf16[64,2432]{1,0:T(8,128)(2,1)S(1)}, u32[]{:S(2)}, u32[]{:S(2)}) collective-permute-start(bf16[64,2432]{1,0:T(8,128)(2,1)S(1)} %shard_map.122.refs_0_), channel_id=1, source_target_pairs={{0,2},{1,9},{2,4},{3,11},{4,6},{5,13},{6,0},{7,15},{8,10},{9,17},{... | collective-permute-start | bytes 933896 | tf_op jit(solution)/shard_map/ppermute | solution.py:32
  16.9 12.4 %collective-permute-start.8 = (bf16[192,2432]{1,0:T(8,128)(2,1)}, bf16[192,2432]{1,0:T(8,128)(2,1)S(1)}, u32[]{:S(2)}, u32[]{:S(2)}) collective-permute-start(bf16[192,2432]{1,0:T(8,128)(2,1)} %bitcast.29), channel_id=1, source_target_pairs={{0,1},{1,0},{2,3},{3,2},{4,5},{5,4},{6,7},{7,6},{8,9},{9,8},{10,11... | collective-permute-start | bytes 2801672 | tf_op jit(solution)/shard_map/ppermute | solution.py:36
  17.6 12.0 %collective-permute-start.7 = (bf16[128,2432]{1,0:T(8,128)(2,1)}, bf16[128,2432]{1,0:T(8,128)(2,1)}, u32[]{:S(2)}, u32[]{:S(2)}) collective-permute-start(bf16[128,2432]{1,0:T(8,128)(2,1)} %get-tuple-element.49.refs_1_), channel_id=1, source_target_pairs={{0,24},{1,7},{2,26},{3,1},{4,28},{5,3},{6,30},{7,5},{8,0},{9,15},{... | collective-permute-start | bytes 1867784 | tf_op jit(solution)/shard_map/ppermute | solution.py:32
  19.5 10.7 %collective-permute-start.6 = (bf16[128,2432]{1,0:T(8,128)(2,1)S(1)}, bf16[128,2432]{1,0:T(8,128)(2,1)}, u32[]{:S(2)}, u32[]{:S(2)}) collective-permute-start(bf16[128,2432]{1,0:T(8,128)(2,1)S(1)} %get-tuple-element.48.refs_0_), channel_id=1, source_target_pairs={{0,8},{1,3},{2,10},{3,5},{4,12},{5,7},{6,14},{7,1},{8,16},{9,11},{... | collective-permute-start | bytes 1867784 | tf_op jit(solution)/shard_map/ppermute | solution.py:32
  19.5 17.4 %collective-permute-start.14 = (bf16[128,2432]{1,0:T(8,128)(2,1)}, bf16[128,2432]{1,0:T(8,128)(2,1)}, u32[]{:S(2)}, u32[]{:S(2)}) collective-permute-start(bf16[128,2432]{1,0:T(8,128)(2,1)} %get-tuple-element.49.refs_1_), channel_id=1, source_target_pairs={{0,8},{1,3},{2,10},{3,5},{4,12},{5,7},{6,14},{7,1},{8,16},{9,11},{... | collective-permute-start | bytes 1867784 | tf_op jit(solution)/shard_map/ppermute | solution.py:32
  19.8 20.6 %collective-permute-start.15 = (bf16[128,2432]{1,0:T(8,128)(2,1)S(1)}, bf16[128,2432]{1,0:T(8,128)(2,1)}, u32[]{:S(2)}, u32[]{:S(2)}) collective-permute-start(bf16[128,2432]{1,0:T(8,128)(2,1)S(1)} %get-tuple-element.48.refs_0_), channel_id=1, source_target_pairs={{0,24},{1,7},{2,26},{3,1},{4,28},{5,3},{6,30},{7,5},{8,0},{9,15},{... | collective-permute-start | bytes 1867784 | tf_op jit(solution)/shard_map/ppermute | solution.py:32
  30.2 16.6 %collective-permute-start.9 = (bf16[128,2432]{1,0:T(8,128)(2,1)}, bf16[128,2432]{1,0:T(8,128)(2,1)S(1)}, u32[]{:S(2)}, u32[]{:S(2)}) collective-permute-start(bf16[128,2432]{1,0:T(8,128)(2,1)} %collective-permute-done.6.refs_2_), channel_id=1, source_target_pairs={{0,8},{1,3},{2,10},{3,5},{4,12},{5,7},{6,14},{7,1},{8,16},{9,11},{... | collective-permute-start | bytes 1867784 | tf_op jit(solution)/shard_map/ppermute | solution.py:32
  30.2 22.9 %collective-permute-start.10 = (bf16[128,2432]{1,0:T(8,128)(2,1)}, bf16[128,2432]{1,0:T(8,128)(2,1)S(1)}, u32[]{:S(2)}, u32[]{:S(2)}) collective-permute-start(bf16[128,2432]{1,0:T(8,128)(2,1)} %collective-permute-done.7.refs_5_), channel_id=1, source_target_pairs={{0,24},{1,7},{2,26},{3,1},{4,28},{5,3},{6,30},{7,5},{8,0},{9,15},{... | collective-permute-start | bytes 1867784 | tf_op jit(solution)/shard_map/ppermute | solution.py:32
  33.2 21.0 %collective-permute-start.5 = (bf16[64,2432]{1,0:T(8,128)(2,1)S(1)}, bf16[64,2432]{1,0:T(8,128)(2,1)S(1)}, u32[]{:S(2)}, u32[]{:S(2)}) collective-permute-start(bf16[64,2432]{1,0:T(8,128)(2,1)S(1)} %shard_map.124), channel_id=1, source_target_pairs={{0,4},{1,17},{2,6},{3,19},{4,0},{5,21},{6,2},{7,23},{8,12},{9,25},... | collective-permute-start | bytes 933896 | tf_op jit(solution)/shard_map/ppermute | solution.py:32
  36.9 17.4 %collective-permute-start.4 = (bf16[64,2432]{1,0:T(8,128)(2,1)S(1)}, bf16[64,2432]{1,0:T(8,128)(2,1)S(1)}, u32[]{:S(2)}, u32[]{:S(2)}) collective-permute-start(bf16[64,2432]{1,0:T(8,128)(2,1)S(1)} %shard_map.124), channel_id=1, source_target_pairs={{0,6},{1,25},{2,0},{3,27},{4,2},{5,29},{6,4},{7,31},{8,14},{9,1},{... | collective-permute-start | bytes 933896 | tf_op jit(solution)/shard_map/ppermute | solution.py:32
  40.4 13.9 %collective-permute-start.3 = (bf16[64,2432]{1,0:T(8,128)(2,1)S(1)}, bf16[64,2432]{1,0:T(8,128)(2,1)S(1)}, u32[]{:S(2)}, u32[]{:S(2)}) collective-permute-start(bf16[64,2432]{1,0:T(8,128)(2,1)S(1)} %shard_map.124), channel_id=1, source_target_pairs={{0,2},{1,9},{2,4},{3,11},{4,6},{5,13},{6,0},{7,15},{8,10},{9,17},{... | collective-permute-start | bytes 933896 | tf_op jit(solution)/shard_map/ppermute | solution.py:32
  46.8 11.3 %collective-permute-start.16 = (bf16[768,256]{1,0:T(8,128)(2,1)S(1)}, bf16[768,256]{1,0:T(8,128)(2,1)S(1)}, u32[]{:S(2)}, u32[]{:S(2)}) collective-permute-start(bf16[768,256]{1,0:T(8,128)(2,1)S(1)} %get-tuple-element.64), channel_id=1, source_target_pairs={{0,1},{1,0},{2,3},{3,2},{4,5},{5,4},{6,7},{7,6},{8,9},{9,8},{10,11... | collective-permute-start | bytes 1179656 | tf_op jit(solution)/shard_map/ppermute | solution.py:36
  54.1 4.0 %collective-permute-start.17 = (bf16[256,256]{1,0:T(8,128)(2,1)S(1)}, bf16[256,256]{1,0:T(8,128)(2,1)S(1)}, u32[]{:S(2)}, u32[]{:S(2)}) collective-permute-start(bf16[256,256]{1,0:T(8,128)(2,1)S(1)} %get-tuple-element.65), channel_id=1, source_target_pairs={{0,1},{1,0},{2,3},{3,2},{4,5},{5,4},{6,7},{7,6},{8,9},{9,8},{10,11... | collective-permute-start | bytes 393224 | tf_op jit(solution)/shard_map/ppermute | solution.py:36
  54.4 119.9 %collective-permute-start.13 = (bf16[256,2432]{1,0:T(8,128)(2,1)S(1)}, bf16[256,2432]{1,0:T(8,128)(2,1)S(1)}, u32[]{:S(2)}, u32[]{:S(2)}) collective-permute-start(bf16[256,2432]{1,0:T(8,128)(2,1)S(1)} %pad_maximum_fusion.refs_0_), channel_id=1, source_target_pairs={{0,16},{1,5},{2,18},{3,7},{4,20},{5,1},{6,22},{7,3},{8,24},{9,13},... | collective-permute-start | bytes 3735560 | tf_op jit(solution)/shard_map/ppermute | solution.py:32
  56.7 117.6 %collective-permute-start.12 = (bf16[256,2432]{1,0:T(8,128)(2,1)S(1)}, bf16[256,2432]{1,0:T(8,128)(2,1)S(1)}, u32[]{:S(2)}, u32[]{:S(2)}) collective-permute-start(bf16[256,2432]{1,0:T(8,128)(2,1)S(1)} %pad_maximum_fusion.refs_0_), channel_id=1, source_target_pairs={{0,24},{1,7},{2,26},{3,1},{4,28},{5,3},{6,30},{7,5},{8,0},{9,15},{... | collective-permute-start | bytes 3735560 | tf_op jit(solution)/shard_map/ppermute | solution.py:32
  57.6 116.7 %collective-permute-start.11 = (bf16[256,2432]{1,0:T(8,128)(2,1)S(1)}, bf16[256,2432]{1,0:T(8,128)(2,1)S(1)}, u32[]{:S(2)}, u32[]{:S(2)}) collective-permute-start(bf16[256,2432]{1,0:T(8,128)(2,1)S(1)} %pad_maximum_fusion.refs_0_), channel_id=1, source_target_pairs={{0,8},{1,3},{2,10},{3,5},{4,12},{5,7},{6,14},{7,1},{8,16},{9,11},{... | collective-permute-start | bytes 3735560 | tf_op jit(solution)/shard_map/ppermute | solution.py:32
  177.4 2.2 collective-permute-start.18
  179.6 133.7 %slice-start = ((s8[9961472]{0:T(1024)(128)(4,1)}), s8[4194304]{0:T(1024)(128)(4,1)S(1)}, s32[]{:S(2)}) async-start(s8[9961472]{0:T(1024)(128)(4,1)} %bitcast.17), calls=%async_computation.1 | async-start | bytes 8388608
  179.6 133.7 %slice-start.1 = ((s8[9961472]{0:T(1024)(128)(4,1)}), s8[4194304]{0:T(1024)(128)(4,1)S(1)}, s32[]{:S(2)}) async-start(s8[9961472]{0:T(1024)(128)(4,1)} %bitcast.17), calls=%async_computation.2 | async-start | bytes 8388608
  179.6 133.7 %slice-start.2 = ((s8[9961472]{0:T(1024)(128)(4,1)}), s8[1572864]{0:T(1024)(128)(4,1)S(1)}, s32[]{:S(2)}) async-start(s8[9961472]{0:T(1024)(128)(4,1)} %bitcast.17), calls=%async_computation.3 | async-start | bytes 3145728
  314.3 16.6 %collective-permute-start.19 = (bf16[2,64,1280]{2,1,0:T(8,128)(2,1)S(1)}, bf16[2,64,1280]{2,1,0:T(8,128)(2,1)S(1)}, u32[]{:S(2)}, u32[]{:S(2)}) collective-permute-start(bf16[2,64,1280]{2,1,0:T(8,128)(2,1)S(1)} %shard_map.132), channel_id=1, source_target_pairs={{0,32},{32,64},{64,96},{96,0},{1,33},{33,65},{65,97},{97,1},{2,34}... | collective-permute-start | bytes 983048 | tf_op jit(solution)/shard_map/ppermute | solution.py:552
  316.6 14.2 %collective-permute-start.20 = (bf16[2,64,1152]{2,1,0:T(8,128)(2,1)S(1)}, bf16[2,64,1152]{2,1,0:T(8,128)(2,1)S(1)}, u32[]{:S(2)}, u32[]{:S(2)}) collective-permute-start(bf16[2,64,1152]{2,1,0:T(8,128)(2,1)S(1)} %shard_map.133), channel_id=1, source_target_pairs={{0,32},{32,64},{64,96},{96,0},{1,33},{33,65},{65,97},{97,1},{2,34}... | collective-permute-start | bytes 884744 | tf_op jit(solution)/shard_map/ppermute | solution.py:552
  (8 other events, 72.7 us)

commit v4 on v3

--- a/solution.py
+++ b/solution.py
@@ -170,7 +170,7 @@
     return front, back, jnp.max(lengths, axis=0, keepdims=True)
 
 
-def prepare_kernel(spots, first, second, third, text, kaug_ref, kv_ref, longest_ref):
+def prepare_kernel(spots, first, second, third, text, kaug_ref, longest_ref):
     lane = lax.broadcasted_iota(jnp.int32, (1, 2 * HD), 1)
     start = 0
     longest = jnp.zeros((1, 2 * HD), jnp.float32)
@@ -182,7 +182,6 @@
             used = lax.broadcasted_iota(jnp.int32, (many, 2 * HD), 0) < spots[pl.program_id(0)]
             last = jnp.where((lane == HD + 3) & jnp.logical_not(used), -30000.0, last)
         front, back, length = widened(kv, lane, last)
-        kv_ref[start : start + many, :] = kv
         kaug_ref[start : start + many, : 2 * HD] = front
         kaug_ref[start : start + many, 2 * HD :] = back
         longest = jnp.maximum(longest, length)
@@ -208,14 +207,13 @@
         prepare_kernel,
         out_shape=(
             jax.ShapeDtypeStruct((branches, rows, 4 * HD), jnp.bfloat16),
-            jax.ShapeDtypeStruct((branches, rows, 2 * HD), jnp.bfloat16),
             jax.ShapeDtypeStruct((branches, 1, 2 * HD), jnp.float32),
         ),
         grid_spec=pltpu.PrefetchScalarGridSpec(
             num_scalar_prefetch=1,
             grid=(branches,),
             in_specs=[stale(1), stale(2), stale(3), each(text.shape[1], 2 * HD)],
-            out_specs=(each(rows, 4 * HD), each(rows, 2 * HD), each(1, 2 * HD)),
+            out_specs=(each(rows, 4 * HD), each(1, 2 * HD)),
         ),
         compiler_params=pltpu.CompilerParams(vmem_limit_bytes=60 * MIB),
         cost_estimate=pl.CostEstimate(
@@ -227,21 +225,36 @@
 def attend_kernel(counts, branch, spots, *refs):
     pieces = refs[: sum(counts)]
     own_pieces, other_pieces = pieces[: counts[0]], pieces[counts[0] :]
-    stale_kaug, stale_kv, stale_longest = refs[sum(counts) : sum(counts) + 3]
+    stale_kaug, stale_longest, cache, text = refs[sum(counts) : sum(counts) + 4]
     out_ref, fresh_ref, kaug, kv_all, qaug, e_scr, total_ref, longest_ref, sems = refs[-9:]
     rows = qaug.shape[0]
     keys = kv_all.shape[0]
-    stale = stale_kv.shape[1]
+    stale = stale_kaug.shape[1]
     lane = lax.broadcasted_iota(jnp.int32, (1, 2 * HD), 1)
 
     chunks = ((0, 2 * rows), (2 * rows, stale // 2), (2 * rows + stale // 2, stale // 2))
     wide_copy = pltpu.make_async_copy(stale_kaug.at[branch], kaug.at[pl.ds(2 * rows, stale), :], sems.at[0])
-    kv_copy = pltpu.make_async_copy(stale_kv.at[branch], kv_all.at[pl.ds(2 * rows, stale), :], sems.at[1])
+    patch = 2 * rows
+    copies = [wide_copy]
+    for i in range(1, 4):
+        at = lax.rem(spots[2 + 2 * CHIPS] + i, 4) * patch
+        copies.append(
+            pltpu.make_async_copy(
+                cache.at[branch, pl.ds(pl.multiple_of(at, patch), patch), :],
+                kv_all.at[pl.ds(i * patch, patch), :],
+                sems.at[i],
+            )
+        )
+    copies.append(
+        pltpu.make_async_copy(
+            text.at[branch], kv_all.at[pl.ds(4 * patch, keys - 4 * patch), :], sems.at[4]
+        )
+    )
 
     @pl.when(pl.program_id(0) == 0)
     def _():
-        wide_copy.start()
-        kv_copy.start()
+        for copy in copies:
+            copy.start()
         start = 0
         longest = stale_longest[...]
         last = jnp.where((lane >= HD) & (lane < HD + 3), 1.0, 0.0)
@@ -312,8 +325,8 @@
 
     @pl.when(pl.program_id(0) == 0)
     def _():
-        wide_copy.wait()
-        kv_copy.wait()
+        for copy in copies:
+            copy.wait()
 
     for chunk in chunks[1:]:
         total = raise_chunk(*chunk, total)
@@ -375,11 +388,11 @@
         out_ref[spots[2 + pl.program_id(0) * CHIPS + block]] = joined.astype(jnp.bfloat16)
 
 
-def attended_rows(spots, branch, own_pieces, other_pieces, prepared, earlier):
+def attended_rows(spots, branch, own_pieces, other_pieces, prepared, cache, text, earlier):
     pieces = (*own_pieces, *other_pieces)
     rows = sum(piece.shape[0] for piece in own_pieces)
     patch = 2 * rows
-    keys = prepared[1].shape[1] + patch
+    keys = prepared[0].shape[1] + patch
 
     def whole(part):
         return pl.BlockSpec(part.shape, lambda i, spots: (0, 0))
@@ -400,9 +413,8 @@
             num_scalar_prefetch=1,
             grid=(2,),
             in_specs=[whole(part) for part in pieces]
-            + [anywhere, anywhere]
-            + [pl.BlockSpec((None, 1, 2 * HD), lambda i, spots: (branch, 0, 0))]
-            + [anywhere] * len(earlier),
+            + [anywhere, pl.BlockSpec((None, 1, 2 * HD), lambda i, spots: (branch, 0, 0))]
+            + [anywhere] * (2 + len(earlier)),
             out_specs=out_specs,
             scratch_shapes=[
                 pltpu.VMEM((keys, 4 * HD), jnp.bfloat16),
@@ -411,15 +423,15 @@
                 pltpu.VMEM((rows, keys), jnp.float32),
                 pltpu.VMEM((rows, 2 * HD), jnp.float32),
                 pltpu.VMEM((1, 2 * HD), jnp.float32),
-                pltpu.SemaphoreType.DMA((2,)),
+                pltpu.SemaphoreType.DMA((5,)),
             ],
         ),
-        input_output_aliases={1 + len(pieces) + 3 + i: i for i in range(len(earlier))},
+        input_output_aliases={1 + len(pieces) + 4 + i: i for i in range(len(earlier))},
         compiler_params=pltpu.CompilerParams(vmem_limit_bytes=48 * MIB),
         cost_estimate=pl.CostEstimate(
             flops=4 * patch * keys * 256, bytes_accessed=8 * MIB, transcendentals=0
         ),
-    )(spots, *pieces, *prepared, *earlier)
+    )(spots, *pieces, *prepared, cache, text, *earlier)
 
 
 def finish_kernel(columns, heads, weight, entering, gate, out_ref, lhs):
@@ -536,11 +548,13 @@
     far_1 = along(line_1, 1, 2)
     own_far, other_far = project([far_low, far_high])
     first = attended_rows(
-        spots, 0, (own_near, own_far), (other_near, other_far), prepared, ()
+        spots, 0, (own_near, own_far), (other_near, other_far), prepared, cache, text, ()
     )
     left_1, right_1, far_1, first = lax.optimization_barrier((left_1, right_1, far_1, first))
     own_all, other_all = project([line_1, left_1, right_1, far_1])
-    attended, fresh = attended_rows(spots, 1, (own_all,), (other_all,), prepared, first)
+    attended, fresh = attended_rows(
+        spots, 1, (own_all,), (other_all,), prepared, cache, text, first
+    )
 
     heads = lax.all_to_all(attended, "seq", split_axis=0, concat_axis=0, tiled=True)
     count = lax.axis_size("section")

time: 332 us -> 334 us (level)
  no operation moved by 1% of the time
where the time goes in v4:
time: 334 us
  Pallas kernels  250 us (75%)
  starting transfers between devices  34.2 us (10%)
  waiting for transfers between devices  18.3 us (5%)
  blocking collectives  17.1 us (5%)
  local copies, waits for them, and re-layouts  5.47 us (2%)
  other arithmetic  4.41 us (1%)
  between operations  4.25 us (1%)
    pallas_call x2, Pallas kernels, attended_rows(): pl.pallas_call(functools.partial(attend_kernel, (len(own_pieces), len(oth...  231 us
    ppermute x15, starting transfers between devices, along(): return lax.ppermute(value, 'seq', pairs_of(phase, step))  24.1 us
    all_to_all x1, blocking collectives, local(): lax.all_to_all(attended, 'seq', split_axis=0, concat_axis=0, tiled=True)  17.1 us
    ppermute x2, waiting for transfers between devices, local(): lax.ppermute(done, 'section', [(i, (i + 1) % count) for i in range(count)])  12.9 us
    pallas_call x3, Pallas kernels, projected_rows(): pl.pallas_call(functools.partial(project_kernel, len(pieces)), out_shape=...  9.31 us
    ppermute x4, starting transfers between devices, swapped(): return lax.ppermute(value, 'seq', [(i, i ^ 1) for i in range(2 * CHIPS)])  7.31 us
  transfers between devices with their start and end apart: 21, of which 6 were waited for; matrix products, arithmetic and copies ran while one was open for 1% of the time, Pallas kernels for 39%

profile of v4, /device:TPU:1, one launch (start us, length us, event | category | flops | bytes accessed | tf_op | source)
XLA Modules:
  0.0 333.9 jit_solution(2376220752565751471)
XLA Ops:
  2.8 4.5 %collective-permute-start.2 = (bf16[64,2432]{1,0:T(8,128)(2,1)S(1)}, bf16[64,2432]{1,0:T(8,128)(2,1)S(1)}, u32[]{:S(2)}, u32[]{:S(2)}) collective-permute-start(bf16[64,2432]{1,0:T(8,128)(2,1)S(1)} %shard_map.122.refs_0_), channel_id=1, source_target_pairs={{0,4},{1,17},{2,6},{3,19},{4,0},{5,21},{6,2},{7,23},{8,12},{9,25},... | collective-permute-start | bytes 933896 | tf_op jit(solution)/shard_map/ppermute | solution.py:32
  9.5 1.3 fusion.4
  14.6 1.3 pad_add_fusion.spots
  16.0 1.1 shard_map.123
  17.8 2.0 collective-permute-start.7
  20.0 2.5 collective-permute-start.15
  22.5 6.0 %shard_map.125 = (bf16[2,6400,256]{2,1,0:T(8,128)(2,1)}, f32[2,1,128]{2,1,0:T(1,128)}) custom-call(s32[35]{0:T(128)} %pad_add_fusion.spots, bf16[2,8192,128]{2,1,0:T(8,128)(2,1)} %bitcast.21, bf16[2,8192,128]{2,1,0:T(8,128)(2,1)} %bitcast.22, bf16[2,8192,128]{2,1,0:T(8,128)(2,1)} %bitcast.23, bf16[2,256,128]{2,1,0:T(8,128)(2,1)} %bitcast.36), custom_call_target="tpu_custom_call" | custom-call | flops 419430400 | bytes 13107200 | tf_op jit(solution)/shard_map/pallas_call | solution.py:206
  28.6 2.0 collective-permute-done.6.refs_2_
  30.7 2.7 collective-permute-start.10
  33.7 3.4 %collective-permute-start.5 = (bf16[64,2432]{1,0:T(8,128)(2,1)S(1)}, bf16[64,2432]{1,0:T(8,128)(2,1)S(1)}, u32[]{:S(2)}, u32[]{:S(2)}) collective-permute-start(bf16[64,2432]{1,0:T(8,128)(2,1)S(1)} %shard_map.124), channel_id=1, source_target_pairs={{0,4},{1,17},{2,6},{3,19},{4,0},{5,21},{6,2},{7,23},{8,12},{9,25},... | collective-permute-start | bytes 933896 | tf_op jit(solution)/shard_map/ppermute | solution.py:32
  37.3 3.7 %collective-permute-start.4 = (bf16[64,2432]{1,0:T(8,128)(2,1)S(1)}, bf16[64,2432]{1,0:T(8,128)(2,1)S(1)}, u32[]{:S(2)}, u32[]{:S(2)}) collective-permute-start(bf16[64,2432]{1,0:T(8,128)(2,1)S(1)} %shard_map.124), channel_id=1, source_target_pairs={{0,6},{1,25},{2,0},{3,27},{4,2},{5,29},{6,4},{7,31},{8,14},{9,1},{... | collective-permute-start | bytes 933896 | tf_op jit(solution)/shard_map/ppermute | solution.py:32
  41.0 5.2 %shard_map.127 = (bf16[768,256]{1,0:T(8,128)(2,1)S(1)}, bf16[768,256]{1,0:T(8,128)(2,1)S(1)}) custom-call(bf16[128,2432]{1,0:T(8,128)(2,1)} %get-tuple-element.46.refs_0_, bf16[128,2432]{1,0:T(8,128)(2,1)} %get-tuple-element.47.refs_1_, bf16[128,2432]{1,0:T(8,128)(2,1)} %collective-permute-done.6.refs_2_, bf16[128,2432]{1,0:T(8,128)(2,1)} %collective-permute-done.14.refs_3_, ...), custom_call_target="tpu_custom_call" | custom-call | flops 1912602624 | bytes 3735552 | tf_op jit(solution)/shard_map/pallas_call | solution.py:149
  47.2 6.3 %collective-permute-start.16 = (bf16[768,256]{1,0:T(8,128)(2,1)S(1)}, bf16[768,256]{1,0:T(8,128)(2,1)S(1)}, u32[]{:S(2)}, u32[]{:S(2)}) collective-permute-start(bf16[768,256]{1,0:T(8,128)(2,1)S(1)} %get-tuple-element.61), channel_id=1, source_target_pairs={{0,1},{1,0},{2,3},{3,2},{4,5},{5,4},{6,7},{7,6},{8,9},{9,8},{10,11... | collective-permute-start | bytes 1179656 | tf_op jit(solution)/shard_map/ppermute | solution.py:36
  54.8 2.3 collective-permute-start.13
  58.6 115.6 %shard_map.129 = (bf16[32,64,128]{2,1,0:T(8,128)(2,1)S(1)}, bf16[2,2048,128]{2,1,0:T(8,128)(2,1)}) custom-call(s32[35]{0:T(128)S(1)} %copy-done.8, bf16[768,256]{1,0:T(8,128)(2,1)S(1)} %get-tuple-element.59.refs_0_, bf16[256,256]{1,0:T(8,128)(2,1)S(1)} %get-tuple-element.60.refs_1_, bf16[768,256]{1,0:T(8,128)(2,1)S(1)} %collective-permute-done.16.refs_2_, ...), custom_call_target="tpu_custom_call" | custom-call | flops 17716740096 | bytes 8388608 | tf_op jit(solution)/shard_map/pallas_call | solution.py:409
  174.3 3.1 shard_map.130
  177.7 1.9 collective-permute-done.18.refs_1_
  180.4 1.2 copy-done.6
  181.6 1.3 copy-done.10
  182.8 115.5 %shard_map.131 = (bf16[32,64,128]{2,1,0:T(8,128)(2,1)S(1)}, bf16[2,2048,128]{2,1,0:T(8,128)(2,1)}) custom-call(s32[35]{0:T(128)S(1)} %copy-done.8, bf16[1024,256]{1,0:T(8,128)(2,1)S(1)} %get-tuple-element.70.refs_0_, bf16[1024,256]{1,0:T(8,128)(2,1)S(1)} %copy-done.10, ...), custom_call_target="tpu_custom_call", output_to_operand_aliasing={{0}: (7, {}), {1}: (8, {})} | custom-call | flops 17716740096 | bytes 8388608 | tf_op jit(solution)/shard_map/pallas_call | solution.py:409
  298.4 17.1 %all_to_all.5.heads = bf16[32,64,128]{2,1,0:T(8,128)(2,1)S(1)} all-to-all(bf16[32,64,128]{2,1,0:T(8,128)(2,1)S(1)} %get-tuple-element.74), channel_id=1, replica_groups=mesh['section'=4,'seq'=32] {'seq'}, dimensions={0} | all-to-all | bytes 1048576 | tf_op jit(solution)/shard_map/all_to_all | solution.py:559
  316.5 1.4 collective-permute-start.19
  318.8 1.4 collective-permute-start.20
  320.2 12.9 %collective-permute-done.20 = bf16[2,64,1152]{2,1,0:T(8,128)(2,1)S(1)} collective-permute-done((bf16[2,64,1152]{2,1,0:T(8,128)(2,1)S(1)}, bf16[2,64,1152]{2,1,0:T(8,128)(2,1)S(1)}, u32[]{:S(2)}, u32[]{:S(2)}) %collective-permute-start.20) | collective-permute-done | bytes 294944 | tf_op jit(solution)/shard_map/ppermute | solution.py:566
  (76 shorter events, 14.4 us)
Async XLA Ops:
  2.8 13.1 %collective-permute-start.2 = (bf16[64,2432]{1,0:T(8,128)(2,1)S(1)}, bf16[64,2432]{1,0:T(8,128)(2,1)S(1)}, u32[]{:S(2)}, u32[]{:S(2)}) collective-permute-start(bf16[64,2432]{1,0:T(8,128)(2,1)S(1)} %shard_map.122.refs_0_), channel_id=1, source_target_pairs={{0,4},{1,17},{2,6},{3,19},{4,0},{5,21},{6,2},{7,23},{8,12},{9,25},... | collective-permute-start | bytes 933896 | tf_op jit(solution)/shard_map/ppermute | solution.py:32
  7.3 8.7 %collective-permute-start.1 = (bf16[64,2432]{1,0:T(8,128)(2,1)S(1)}, bf16[64,2432]{1,0:T(8,128)(2,1)S(1)}, u32[]{:S(2)}, u32[]{:S(2)}) collective-permute-start(bf16[64,2432]{1,0:T(8,128)(2,1)S(1)} %shard_map.122.refs_0_), channel_id=1, source_target_pairs={{0,6},{1,25},{2,0},{3,27},{4,2},{5,29},{6,4},{7,31},{8,14},{9,1},{... | collective-permute-start | bytes 933896 | tf_op jit(solution)/shard_map/ppermute | solution.py:32
  7.8 8.3 %collective-permute-start = (bf16[64,2432]{1,0:T(8,128)(2,1)S(1)}, bf16[64,2432]{1,0:T(8,128)(2,1)S(1)}, u32[]{:S(2)}, u32[]{:S(2)}) collective-permute-start(bf16[64,2432]{1,0:T(8,128)(2,1)S(1)} %shard_map.122.refs_0_), channel_id=1, source_target_pairs={{0,2},{1,9},{2,4},{3,11},{4,6},{5,13},{6,0},{7,15},{8,10},{9,17},{... | collective-permute-start | bytes 933896 | tf_op jit(solution)/shard_map/ppermute | solution.py:32
  17.1 11.3 %collective-permute-start.8 = (bf16[192,2432]{1,0:T(8,128)(2,1)S(1)}, bf16[192,2432]{1,0:T(8,128)(2,1)S(1)}, u32[]{:S(2)}, u32[]{:S(2)}) collective-permute-start(bf16[192,2432]{1,0:T(8,128)(2,1)S(1)} %bitcast.34), channel_id=1, source_target_pairs={{0,1},{1,0},{2,3},{3,2},{4,5},{5,4},{6,7},{7,6},{8,9},{9,8},{10,11... | collective-permute-start | bytes 2801672 | tf_op jit(solution)/shard_map/ppermute | solution.py:36
  17.8 10.8 %collective-permute-start.7 = (bf16[128,2432]{1,0:T(8,128)(2,1)}, bf16[128,2432]{1,0:T(8,128)(2,1)S(1)}, u32[]{:S(2)}, u32[]{:S(2)}) collective-permute-start(bf16[128,2432]{1,0:T(8,128)(2,1)} %get-tuple-element.47.refs_1_), channel_id=1, source_target_pairs={{0,24},{1,7},{2,26},{3,1},{4,28},{5,3},{6,30},{7,5},{8,0},{9,15},{... | collective-permute-start | bytes 1867784 | tf_op jit(solution)/shard_map/ppermute | solution.py:32
  19.8 10.9 %collective-permute-start.6 = (bf16[128,2432]{1,0:T(8,128)(2,1)}, bf16[128,2432]{1,0:T(8,128)(2,1)}, u32[]{:S(2)}, u32[]{:S(2)}) collective-permute-start(bf16[128,2432]{1,0:T(8,128)(2,1)} %get-tuple-element.46.refs_0_), channel_id=1, source_target_pairs={{0,8},{1,3},{2,10},{3,5},{4,12},{5,7},{6,14},{7,1},{8,16},{9,11},{... | collective-permute-start | bytes 1867784 | tf_op jit(solution)/shard_map/ppermute | solution.py:32
  19.8 17.6 %collective-permute-start.14 = (bf16[128,2432]{1,0:T(8,128)(2,1)}, bf16[128,2432]{1,0:T(8,128)(2,1)}, u32[]{:S(2)}, u32[]{:S(2)}) collective-permute-start(bf16[128,2432]{1,0:T(8,128)(2,1)} %get-tuple-element.47.refs_1_), channel_id=1, source_target_pairs={{0,8},{1,3},{2,10},{3,5},{4,12},{5,7},{6,14},{7,1},{8,16},{9,11},{... | collective-permute-start | bytes 1867784 | tf_op jit(solution)/shard_map/ppermute | solution.py:32
  20.0 21.0 %collective-permute-start.15 = (bf16[128,2432]{1,0:T(8,128)(2,1)}, bf16[128,2432]{1,0:T(8,128)(2,1)}, u32[]{:S(2)}, u32[]{:S(2)}) collective-permute-start(bf16[128,2432]{1,0:T(8,128)(2,1)} %get-tuple-element.46.refs_0_), channel_id=1, source_target_pairs={{0,24},{1,7},{2,26},{3,1},{4,28},{5,3},{6,30},{7,5},{8,0},{9,15},{... | collective-permute-start | bytes 1867784 | tf_op jit(solution)/shard_map/ppermute | solution.py:32
  30.7 16.6 %collective-permute-start.9 = (bf16[128,2432]{1,0:T(8,128)(2,1)}, bf16[128,2432]{1,0:T(8,128)(2,1)S(1)}, u32[]{:S(2)}, u32[]{:S(2)}) collective-permute-start(bf16[128,2432]{1,0:T(8,128)(2,1)} %collective-permute-done.6.refs_2_), channel_id=1, source_target_pairs={{0,8},{1,3},{2,10},{3,5},{4,12},{5,7},{6,14},{7,1},{8,16},{9,11},{... | collective-permute-start | bytes 1867784 | tf_op jit(solution)/shard_map/ppermute | solution.py:32
  30.7 22.8 %collective-permute-start.10 = (bf16[128,2432]{1,0:T(8,128)(2,1)S(1)}, bf16[128,2432]{1,0:T(8,128)(2,1)S(1)}, u32[]{:S(2)}, u32[]{:S(2)}) collective-permute-start(bf16[128,2432]{1,0:T(8,128)(2,1)S(1)} %collective-permute-done.7.refs_5_), channel_id=1, source_target_pairs={{0,24},{1,7},{2,26},{3,1},{4,28},{5,3},{6,30},{7,5},{8,0},{9,15},{... | collective-permute-start | bytes 1867784 | tf_op jit(solution)/shard_map/ppermute | solution.py:32
  33.7 21.0 %collective-permute-start.5 = (bf16[64,2432]{1,0:T(8,128)(2,1)S(1)}, bf16[64,2432]{1,0:T(8,128)(2,1)S(1)}, u32[]{:S(2)}, u32[]{:S(2)}) collective-permute-start(bf16[64,2432]{1,0:T(8,128)(2,1)S(1)} %shard_map.124), channel_id=1, source_target_pairs={{0,4},{1,17},{2,6},{3,19},{4,0},{5,21},{6,2},{7,23},{8,12},{9,25},... | collective-permute-start | bytes 933896 | tf_op jit(solution)/shard_map/ppermute | solution.py:32
  37.3 17.4 %collective-permute-start.4 = (bf16[64,2432]{1,0:T(8,128)(2,1)S(1)}, bf16[64,2432]{1,0:T(8,128)(2,1)S(1)}, u32[]{:S(2)}, u32[]{:S(2)}) collective-permute-start(bf16[64,2432]{1,0:T(8,128)(2,1)S(1)} %shard_map.124), channel_id=1, source_target_pairs={{0,6},{1,25},{2,0},{3,27},{4,2},{5,29},{6,4},{7,31},{8,14},{9,1},{... | collective-permute-start | bytes 933896 | tf_op jit(solution)/shard_map/ppermute | solution.py:32
  41.0 13.7 %collective-permute-start.3 = (bf16[64,2432]{1,0:T(8,128)(2,1)S(1)}, bf16[64,2432]{1,0:T(8,128)(2,1)S(1)}, u32[]{:S(2)}, u32[]{:S(2)}) collective-permute-start(bf16[64,2432]{1,0:T(8,128)(2,1)S(1)} %shard_map.124), channel_id=1, source_target_pairs={{0,2},{1,9},{2,4},{3,11},{4,6},{5,13},{6,0},{7,15},{8,10},{9,17},{... | collective-permute-start | bytes 933896 | tf_op jit(solution)/shard_map/ppermute | solution.py:32
  47.2 11.4 %collective-permute-start.16 = (bf16[768,256]{1,0:T(8,128)(2,1)S(1)}, bf16[768,256]{1,0:T(8,128)(2,1)S(1)}, u32[]{:S(2)}, u32[]{:S(2)}) collective-permute-start(bf16[768,256]{1,0:T(8,128)(2,1)S(1)} %get-tuple-element.61), channel_id=1, source_target_pairs={{0,1},{1,0},{2,3},{3,2},{4,5},{5,4},{6,7},{7,6},{8,9},{9,8},{10,11... | collective-permute-start | bytes 1179656 | tf_op jit(solution)/shard_map/ppermute | solution.py:36
  54.6 4.0 %collective-permute-start.17 = (bf16[256,256]{1,0:T(8,128)(2,1)S(1)}, bf16[256,256]{1,0:T(8,128)(2,1)S(1)}, u32[]{:S(2)}, u32[]{:S(2)}) collective-permute-start(bf16[256,256]{1,0:T(8,128)(2,1)S(1)} %get-tuple-element.62), channel_id=1, source_target_pairs={{0,1},{1,0},{2,3},{3,2},{4,5},{5,4},{6,7},{7,6},{8,9},{9,8},{10,11... | collective-permute-start | bytes 393224 | tf_op jit(solution)/shard_map/ppermute | solution.py:36
  54.8 119.4 %collective-permute-start.13 = (bf16[256,2432]{1,0:T(8,128)(2,1)S(1)}, bf16[256,2432]{1,0:T(8,128)(2,1)S(1)}, u32[]{:S(2)}, u32[]{:S(2)}) collective-permute-start(bf16[256,2432]{1,0:T(8,128)(2,1)S(1)} %pad_maximum_fusion.refs_0_), channel_id=1, source_target_pairs={{0,16},{1,5},{2,18},{3,7},{4,20},{5,1},{6,22},{7,3},{8,24},{9,13},... | collective-permute-start | bytes 3735560 | tf_op jit(solution)/shard_map/ppermute | solution.py:32
  57.1 117.1 %collective-permute-start.12 = (bf16[256,2432]{1,0:T(8,128)(2,1)S(1)}, bf16[256,2432]{1,0:T(8,128)(2,1)S(1)}, u32[]{:S(2)}, u32[]{:S(2)}) collective-permute-start(bf16[256,2432]{1,0:T(8,128)(2,1)S(1)} %pad_maximum_fusion.refs_0_), channel_id=1, source_target_pairs={{0,24},{1,7},{2,26},{3,1},{4,28},{5,3},{6,30},{7,5},{8,0},{9,15},{... | collective-permute-start | bytes 3735560 | tf_op jit(solution)/shard_map/ppermute | solution.py:32
  58.0 116.2 %collective-permute-start.11 = (bf16[256,2432]{1,0:T(8,128)(2,1)S(1)}, bf16[256,2432]{1,0:T(8,128)(2,1)S(1)}, u32[]{:S(2)}, u32[]{:S(2)}) collective-permute-start(bf16[256,2432]{1,0:T(8,128)(2,1)S(1)} %pad_maximum_fusion.refs_0_), channel_id=1, source_target_pairs={{0,8},{1,3},{2,10},{3,5},{4,12},{5,7},{6,14},{7,1},{8,16},{9,11},{... | collective-permute-start | bytes 3735560 | tf_op jit(solution)/shard_map/ppermute | solution.py:32
  177.4 2.2 collective-permute-start.18
  180.4 135.1 %slice-start = ((s8[9961472]{0:T(1024)(128)(4,1)}), s8[4194304]{0:T(1024)(128)(4,1)S(1)}, s32[]{:S(2)}) async-start(s8[9961472]{0:T(1024)(128)(4,1)} %bitcast.17), calls=%async_computation.1 | async-start | bytes 8388608
  182.8 132.6 %slice-start.1 = ((s8[9961472]{0:T(1024)(128)(4,1)}), s8[4194304]{0:T(1024)(128)(4,1)S(1)}, s32[]{:S(2)}) async-start(s8[9961472]{0:T(1024)(128)(4,1)} %bitcast.17), calls=%async_computation.2 | async-start | bytes 8388608
  182.8 132.6 %slice-start.2 = ((s8[9961472]{0:T(1024)(128)(4,1)}), s8[1572864]{0:T(1024)(128)(4,1)S(1)}, s32[]{:S(2)}) async-start(s8[9961472]{0:T(1024)(128)(4,1)} %bitcast.17), calls=%async_computation.3 | async-start | bytes 3145728
  316.5 16.6 %collective-permute-start.19 = (bf16[2,64,1280]{2,1,0:T(8,128)(2,1)S(1)}, bf16[2,64,1280]{2,1,0:T(8,128)(2,1)S(1)}, u32[]{:S(2)}, u32[]{:S(2)}) collective-permute-start(bf16[2,64,1280]{2,1,0:T(8,128)(2,1)S(1)} %shard_map.132), channel_id=1, source_target_pairs={{0,32},{32,64},{64,96},{96,0},{1,33},{33,65},{65,97},{97,1},{2,34}... | collective-permute-start | bytes 983048 | tf_op jit(solution)/shard_map/ppermute | solution.py:566
  318.8 14.2 %collective-permute-start.20 = (bf16[2,64,1152]{2,1,0:T(8,128)(2,1)S(1)}, bf16[2,64,1152]{2,1,0:T(8,128)(2,1)S(1)}, u32[]{:S(2)}, u32[]{:S(2)}) collective-permute-start(bf16[2,64,1152]{2,1,0:T(8,128)(2,1)S(1)} %shard_map.133), channel_id=1, source_target_pairs={{0,32},{32,64},{64,96},{96,0},{1,33},{33,65},{65,97},{97,1},{2,34}... | collective-permute-start | bytes 884744 | tf_op jit(solution)/shard_map/ppermute | solution.py:566
  (13 other events, 72.1 us)
